TPU v7x, 32 devices: a whole 2x2x4 slice. The times are simulated.
32 devices in a mesh: gx: 4 (over x, core), gy: 2 (over y), gz: 4 (over z).
Axes of the slice: x: 2, y: 2, z: 4, core: 2. Of those that a mesh axis runs over, the one named last changes fastest.
Arguments:
- source: float32 [32, 32, 512], P('gx', 'gy', 'gz'), may hold values from -6 to 6
- state: float32 [32, 32, 512], P('gx', 'gy', 'gz'), may hold values from -6 to 6
- log_coef: float32 [32, 32, 512], P('gx', 'gy', 'gz'), may hold values from -1 to 1
- lateral: float32 [32, 32], P('gx', 'gy'), may hold values from -0.5 to 0.5
- owners: int32 [4, 2, 4], P('gx', 'gy'), may hold values from 0 to 3, as said below
Outputs:
- adjoint_field: float32 [32, 32, 512], P('gx', 'gy', 'gz')
- lateral_gradient: float32 [32, 32], P('gx', ('gy', 'gz'))
Inputs may be any that keep to these rules, and one draw needn't show every extreme that they name: Along each line, the devices with equal owners entries form a contiguous run of at most 2 devices, and every line has a run of exactly 2; the entry names the device that solves that run's level-2 system, which need not belong to the run; different runs of a line name different devices.
All inputs are finite; a program needn't handle non-finite values.
Results may differ from a plain program's by a relative error of at most 0.0003.
Values sent between devices are 32-bit elements; how exact they have to be, the bound alone decides.
A program may use at most 64 MiB of HBM per device.

v0:
```python
import math

import jax
import jax.numpy as jnp
from jax import lax
from jax.sharding import PartitionSpec as P

SWEEPS = 3
ANISO = 200


omega_relax = 0.8
neighbour_offsets = ((2, 1, 1), (0, 1, 1), (1, 2, 1), (1, 0, 1), (1, 1, 2), (1, 1, 0))


def padded_2(value, sides, width):
    for axis, dim in sides:
        count, length = (lax.axis_size(axis), value.shape[dim])
        up = [(i, (i + 1) % count) for i in range(count - 1)]
        down = [(j, i) for i, j in up]
        last = lax.slice_in_dim(value, length - width, length, axis=dim)
        first = lax.slice_in_dim(value, 0, width, axis=dim)
        before = lax.ppermute(last, axis, up)
        after = lax.ppermute(first, axis, down)
        value = jnp.concatenate([before, value, after], axis=dim)
    return value


def neighbour(padded, offset, shape):
    return padded[
        offset[0] : offset[0] + shape[0],
        offset[1] : offset[1] + shape[1],
        offset[2] : offset[2] + shape[2],
    ]


def face_scale(scale, order_index):
    if order_index >= 4:
        return scale * ANISO
    return scale


def halo_fine(field):
    return padded_2(field, (("gx", 0), ("gy", 1), ("gz", 2)), 1)


def halo_mid(field):
    return padded_2(field, (("gx", 0), ("gy", 1), ("gz", 2)), 1)


def level_weights(padded, coef, scale):
    weights = []
    for order_index, offset in enumerate(neighbour_offsets):
        raw = neighbour(padded, offset, coef.shape)
        fixed = jnp.where(raw == 0.0, coef, raw)
        weights.append(face_scale(scale, order_index) * (0.5 * (coef + fixed)))
    total = weights[0]
    for extra in weights[1:]:
        total = total + extra
    return (weights, total)


def operate(padded, field, weights, total):
    result = total * field
    for order_index, offset in enumerate(neighbour_offsets):
        result = result - weights[order_index] * neighbour(padded, offset, field.shape)
    return result


def smooth(field, rhs, weights, total, halo_step, from_zero):
    remaining = SWEEPS
    if from_zero:
        field = omega_relax * rhs / total
        remaining = SWEEPS - 1
    for repeat in range(remaining):
        padded = halo_step(field)
        field = field + omega_relax * (rhs - operate(padded, field, weights, total)) / total
    return field


def restrict(field):
    shape = field.shape
    return field.reshape(shape[0] // 2, 2, shape[1] // 2, 2, shape[2] // 2, 2).mean(axis=(1, 3, 5))


def prolong(field):
    shape = field.shape
    spread = jnp.broadcast_to(
        field[:, None, :, None, :, None], (shape[0], 2, shape[1], 2, shape[2], 2)
    )
    return spread.reshape(2 * shape[0], 2 * shape[1], 2 * shape[2])


def line_solve(rhs, total, lower):
    upper = jnp.concatenate([lower[..., 1:], jnp.zeros_like(lower[..., :1])], axis=-1)
    solved = lax.linalg.tridiagonal_solve(-lower, total, -upper, rhs[..., None])
    return solved[..., 0]


def per_device(source, state, log_coef, lateral, owners):
    coef = jnp.exp(log_coef + lateral[:, :, None])
    mid_coef = restrict(coef)
    low_coef = restrict(mid_coef)
    low_pad = padded_2(low_coef, (("gx", 0), ("gy", 1), ("gz", 2)), 1)
    low_weights, low_total = level_weights(low_pad, low_coef, 0.0625)
    coef_pad = halo_fine(coef)
    fine_weights, fine_total = level_weights(coef_pad, coef, 1.0)
    mid_weights, mid_total = level_weights(halo_mid(mid_coef), mid_coef, 0.25)
    adjoint = smooth(jnp.zeros_like(source), source, fine_weights, fine_total, halo_fine, True)
    mid_rhs = restrict(source - operate(halo_fine(adjoint), adjoint, fine_weights, fine_total))
    mid_field = smooth(jnp.zeros_like(mid_rhs), mid_rhs, mid_weights, mid_total, halo_mid, True)
    low_rhs = restrict(mid_rhs - operate(halo_mid(mid_field), mid_field, mid_weights, mid_total))
    position = lax.axis_index("gz")
    count = lax.axis_size("gz")
    depth_len = low_coef.shape[2]
    line = owners[0, 0]
    own_group = line[position]
    prev_group = line[jnp.maximum(position - 1, 0)]
    cut_first = (position == 0) | (own_group != prev_group)
    depth_first = (jnp.arange(depth_len) == 0)[None, None, :]
    lower = jnp.where(cut_first & depth_first, jnp.zeros_like(low_weights[5]), low_weights[5])
    slots = jnp.arange(count)
    target = (slots == own_group).astype(jnp.float32)
    member = (line == position).astype(jnp.float32)
    piece = jnp.stack([low_rhs, low_total, lower])
    outgoing = piece[:, :, :, None, :] * target[None, None, None, :, None]
    received = lax.all_to_all(outgoing, "gz", split_axis=3, concat_axis=3, tiled=True)
    flat = (received.shape[1], received.shape[2], count * received.shape[4])
    diag_flat = (received[1] + (1.0 - member)[None, None, :, None]).reshape(flat)
    solution = line_solve(received[0].reshape(flat), diag_flat, received[2].reshape(flat))
    returned = lax.all_to_all(
        solution.reshape(received.shape[1:]), "gz", split_axis=2, concat_axis=2, tiled=True
    )
    correction = jnp.sum(returned, axis=2)
    mid_field = smooth(
        mid_field + prolong(correction), mid_rhs, mid_weights, mid_total, halo_mid, False
    )
    adjoint = smooth(
        adjoint + prolong(mid_field), source, fine_weights, fine_total, halo_fine, False
    )
    paired = padded_2(jnp.stack([adjoint, state]), (("gx", 1), ("gy", 2), ("gz", 3)), 1)
    adjoint_pad, state_pad = (paired[0], paired[1])
    grad_terms = jnp.zeros_like(adjoint)
    for offset in neighbour_offsets:
        raw = neighbour(coef_pad, offset, coef.shape)
        factor = jnp.where(raw == 0.0, 1.0, 0.5)
        grad_terms = grad_terms + factor * (
            adjoint - neighbour(adjoint_pad, offset, adjoint.shape)
        ) * (state - neighbour(state_pad, offset, state.shape))
    partial_sums = jnp.sum(coef * grad_terms, axis=2)
    summed = lax.psum_scatter(partial_sums, "gz", scatter_dimension=1, tiled=True)
    return (adjoint, summed * (-1.0 / math.sqrt(source.shape[2] * count)))


def solution(mesh):
    placed = (
        P("gx", "gy", "gz"),
        P("gx", "gy", "gz"),
        P("gx", "gy", "gz"),
        P("gx", "gy"),
        P("gx", "gy", None),
    )
    return jax.shard_map(
        per_device,
        mesh=mesh,
        in_specs=placed,
        out_specs=(P("gx", "gy", "gz"), P("gx", ("gy", "gz"))),
        check_vma=False,
    )
```

profile of v0, /device:TPU:0, one launch (start us, length us, event | category | flops | bytes accessed | tf_op | source)
XLA Modules:
  0.0 450.4 jit_solution(1129678054179860084)
XLA Ops:
  8.0 4.9 %collective-permute-start.3 = (f32[10,1,128]{2,1,0:T(1,128)S(1)}, f32[10,1,128]{2,1,0:T(1,128)S(1)}, u32[]{:S(2)}, u32[]{:S(2)}) collective-permute-start(f32[10,1,128]{2,1,0:T(1,128)S(1)} %get-tuple-element.549), channel_id=1, source_target_pairs={{0,4},{1,5},{2,6},{3,7},{8,12},{9,13},{10,14},{11,15},{16,20},{17,... | collective-permute-start | bytes 15368 | tf_op jit(solution)/shard_map/ppermute | solution.py:23
  15.7 5.2 %collective-permute-start.5 = (f32[10,18,1]{2,1,0:T(8,128)S(1)}, f32[10,18,1]{2,1,0:T(8,128)S(1)}, u32[]{:S(2)}, u32[]{:S(2)}) collective-permute-start(f32[10,18,1]{2,1,0:T(8,128)S(1)} %get-tuple-element.534), channel_id=1, source_target_pairs={{0,1},{1,2},{2,3},{4,5},{5,6},{6,7},{8,9},{9,10},{10,11},{12,13},{... | collective-permute-start | bytes 2168 | tf_op jit(solution)/shard_map/ppermute | solution.py:23
  38.5 5.2 %collective-permute-start.11 = (f32[10,18,1]{2,1,0:T(8,128)S(1)}, f32[10,18,1]{2,1,0:T(8,128)S(1)}, u32[]{:S(2)}, u32[]{:S(2)}) collective-permute-start(f32[10,18,1]{2,1,0:T(8,128)S(1)} %get-tuple-element.533), channel_id=1, source_target_pairs={{0,1},{1,2},{2,3},{4,5},{5,6},{6,7},{8,9},{9,10},{10,11},{12,13},{... | collective-permute-start | bytes 2168 | tf_op jit(solution)/shard_map/ppermute | solution.py:23
  43.6 5.5 %reshape.511 = f32[4,2,8,2,64,2]{5,4,3,2,1,0:T(8,128)} reshape(f32[8,16,128]{2,1,0:T(8,128)S(1)} %add_exponential_fusion) | data formatting | bytes 131072 | tf_op jit(solution)/shard_map/reshape | solution.py:83
  65.1 5.6 %collective-permute-start.25 = (f32[1,8,64]{2,1,0:T(8,128)S(1)}, f32[1,8,64]{2,1,0:T(8,128)S(1)}, u32[]{:S(2)}, u32[]{:S(2)}) collective-permute-start(f32[1,8,64]{2,1,0:T(8,128)S(1)} %get-tuple-element.607), channel_id=1, source_target_pairs={{0,8},{8,16},{16,24},{1,9},{9,17},{17,25},{2,10},{10,18},{18,26},{... | collective-permute-start | bytes 6152 | tf_op jit(solution)/shard_map/ppermute | solution.py:23
  100.4 4.7 %collective-permute-start.23 = (f32[10,18,1]{2,1,0:T(8,128)S(1)}, f32[10,18,1]{2,1,0:T(8,128)S(1)}, u32[]{:S(2)}, u32[]{:S(2)}) collective-permute-start(f32[10,18,1]{2,1,0:T(8,128)S(1)} %get-tuple-element.529), channel_id=1, source_target_pairs={{0,1},{1,2},{2,3},{4,5},{5,6},{6,7},{8,9},{9,10},{10,11},{12,13},{... | collective-permute-start | bytes 2168 | tf_op jit(solution)/shard_map/ppermute | solution.py:23
  111.2 5.5 %reshape.510 = f32[4,2,8,2,64,2]{5,4,3,2,1,0:T(8,128)} reshape(f32[8,16,128]{2,1,0:T(8,128)S(1)} %fusion.427) | data formatting | bytes 131072 | tf_op jit(solution)/shard_map/reshape | solution.py:83
  160.7 5.0 %collective-permute-start.41 = (f32[6,10,1]{2,1,0:T(8,128)S(1)}, f32[6,10,1]{2,1,0:T(8,128)S(1)}, u32[]{:S(2)}, u32[]{:S(2)}) collective-permute-start(f32[6,10,1]{2,1,0:T(8,128)S(1)} %get-tuple-element.576), channel_id=1, source_target_pairs={{0,1},{1,2},{2,3},{4,5},{5,6},{6,7},{8,9},{9,10},{10,11},{12,13},{... | collective-permute-start | bytes 728 | tf_op jit(solution)/shard_map/ppermute | solution.py:23
  173.4 5.0 %collective-permute-start.53 = (f32[4,6,1]{2,0,1:T(4,128)S(1)}, f32[4,6,1]{2,0,1:T(4,128)S(1)}, u32[]{:S(2)}, u32[]{:S(2)}) collective-permute-start(f32[4,6,1]{2,0,1:T(4,128)S(1)} %get-tuple-element.612), channel_id=1, source_target_pairs={{0,1},{1,2},{2,3},{4,5},{5,6},{6,7},{8,9},{9,10},{10,11},{12,13},{... | collective-permute-start | bytes 296 | tf_op jit(solution)/shard_map/ppermute | solution.py:23
  194.9 6.9 %all-to-all-start = ((f32[4,1,768]{2,1,0:T(1,128)}), f32[4,1,768]{2,1,0:T(1,128)S(1)}, u32[]{:S(2)}, u32[]{:S(2)}) async-start(f32[4,1,768]{2,1,0:T(1,128)} %reshape.619), calls=%async_computation | async-start | bytes 24576 | tf_op jit(solution)/shard_map/all_to_all | solution.py:127
  202.0 5.4 %all-to-all-done = f32[4,1,768]{2,1,0:T(1,128)S(1)} async-done(((f32[4,1,768]{2,1,0:T(1,128)}), f32[4,1,768]{2,1,0:T(1,128)S(1)}, u32[]{:S(2)}, u32[]{:S(2)}) %all-to-all-start) | async-done | bytes 12320 | tf_op jit(solution)/shard_map/all_to_all | solution.py:127
  210.3 21.7 %while.32 = (s32[]{:T(128)}, f32[2,4]{1,0:T(2,128)S(1)}, f32[2,4,1]{1,0,2:T(2,128)S(1)}, f32[3,32,2,4]{1,0,3,2:T(4,128)S(1)}, f32[3,32,2,4,1]{1,0,3,2,4:T(4,128)...) while((s32[]{:T(128)}, f32[2,4]{1,0:T(2,128)S(1)}, ...), condition=%wide.region_5.6_spmd, body=%wide.region_4.5_spmd.sunk | while | flops 1585 | bytes 19529 | solution.py:96
  240.2 10.7 %while.33 = (s32[]{:T(128)}, f32[2,4,1]{1,0,2:T(2,128)S(1)}, f32[3,32,2,4,1]{1,0,3,2,4:T(4,128)S(1)}, f32[3,32,2,4,1]{3,2,4,1,0:T(2,128)S(1)}, f32[3,32,2,4]{3,2...) while((s32[]{:T(128)}, f32[2,4,1]{1,0,2:T(2,128)S(1)}, ...), condition=%wide.region_7.8_spmd, body=%wide.region_6.7_spmd.sunk | while | flops 546 | bytes 10161 | solution.py:96
  254.8 7.9 %all_to_all.10 = f32[4,1,256]{2,1,0:T(1,128)S(1)} all-to-all(f32[4,1,256]{2,1,0:T(1,128)S(1)} %reshape.621), channel_id=1, replica_groups=mesh['gx'=4,'gy'=2,'gz'=4] {'gz'}, dimensions={0} | all-to-all | bytes 8192 | tf_op jit(solution)/shard_map/all_to_all | solution.py:131
  298.1 5.0 %collective-permute-start.65 = (f32[6,10,1]{2,1,0:T(8,128)S(1)}, f32[6,10,1]{2,1,0:T(8,128)S(1)}, u32[]{:S(2)}, u32[]{:S(2)}) collective-permute-start(f32[6,10,1]{2,1,0:T(8,128)S(1)} %get-tuple-element.567), channel_id=1, source_target_pairs={{0,1},{1,2},{2,3},{4,5},{5,6},{6,7},{8,9},{9,10},{10,11},{12,13},{... | collective-permute-start | bytes 728 | tf_op jit(solution)/shard_map/ppermute | solution.py:23
  319.7 4.6 %collective-permute-start.71 = (f32[6,10,1]{2,1,0:T(8,128)S(1)}, f32[6,10,1]{2,1,0:T(8,128)S(1)}, u32[]{:S(2)}, u32[]{:S(2)}) collective-permute-start(f32[6,10,1]{2,1,0:T(8,128)S(1)} %get-tuple-element.565), channel_id=1, source_target_pairs={{0,1},{1,2},{2,3},{4,5},{5,6},{6,7},{8,9},{9,10},{10,11},{12,13},{... | collective-permute-start | bytes 728 | tf_op jit(solution)/shard_map/ppermute | solution.py:23
  334.0 5.0 %collective-permute-start.73 = (f32[1,16,128]{2,1,0:T(8,128)S(1)}, f32[1,16,128]{2,1,0:T(8,128)S(1)}, u32[]{:S(2)}, u32[]{:S(2)}) collective-permute-start(f32[1,16,128]{2,1,0:T(8,128)S(1)} %get-tuple-element.554), channel_id=1, source_target_pairs={{0,8},{8,16},{16,24},{1,9},{9,17},{17,25},{2,10},{10,18},{18,26},{... | collective-permute-start | bytes 24584 | tf_op jit(solution)/shard_map/ppermute | solution.py:23
  348.5 4.6 %collective-permute-start.77 = (f32[10,18,1]{2,1,0:T(8,128)S(1)}, f32[10,18,1]{2,1,0:T(8,128)S(1)}, u32[]{:S(2)}, u32[]{:S(2)}) collective-permute-start(f32[10,18,1]{2,1,0:T(8,128)S(1)} %get-tuple-element.527), channel_id=1, source_target_pairs={{0,1},{1,2},{2,3},{4,5},{5,6},{6,7},{8,9},{9,10},{10,11},{12,13},{... | collective-permute-start | bytes 2168 | tf_op jit(solution)/shard_map/ppermute | solution.py:23
  357.0 5.1 %collective-permute-start.79 = (f32[1,16,128]{2,1,0:T(8,128)S(1)}, f32[1,16,128]{2,1,0:T(8,128)S(1)}, u32[]{:S(2)}, u32[]{:S(2)}) collective-permute-start(f32[1,16,128]{2,1,0:T(8,128)S(1)} %get-tuple-element.552), channel_id=1, source_target_pairs={{0,8},{8,16},{16,24},{1,9},{9,17},{17,25},{2,10},{10,18},{18,26},{... | collective-permute-start | bytes 24584 | tf_op jit(solution)/shard_map/ppermute | solution.py:23
  371.5 4.7 %collective-permute-start.83 = (f32[10,18,1]{2,1,0:T(8,128)S(1)}, f32[10,18,1]{2,1,0:T(8,128)S(1)}, u32[]{:S(2)}, u32[]{:S(2)}) collective-permute-start(f32[10,18,1]{2,1,0:T(8,128)S(1)} %get-tuple-element.525), channel_id=1, source_target_pairs={{0,1},{1,2},{2,3},{4,5},{5,6},{6,7},{8,9},{9,10},{10,11},{12,13},{... | collective-permute-start | bytes 2168 | tf_op jit(solution)/shard_map/ppermute | solution.py:23
  380.1 5.1 %collective-permute-start.85 = (f32[1,16,128]{2,1,0:T(8,128)S(1)}, f32[1,16,128]{2,1,0:T(8,128)S(1)}, u32[]{:S(2)}, u32[]{:S(2)}) collective-permute-start(f32[1,16,128]{2,1,0:T(8,128)S(1)} %get-tuple-element.550), channel_id=1, source_target_pairs={{0,8},{8,16},{16,24},{1,9},{9,17},{17,25},{2,10},{10,18},{18,26},{... | collective-permute-start | bytes 24584 | tf_op jit(solution)/shard_map/ppermute | solution.py:23
  394.6 4.7 %collective-permute-start.89 = (f32[10,18,1]{2,1,0:T(8,128)S(1)}, f32[10,18,1]{2,1,0:T(8,128)S(1)}, u32[]{:S(2)}, u32[]{:S(2)}) collective-permute-start(f32[10,18,1]{2,1,0:T(8,128)S(1)} %get-tuple-element.523), channel_id=1, source_target_pairs={{0,1},{1,2},{2,3},{4,5},{5,6},{6,7},{8,9},{9,10},{10,11},{12,13},{... | collective-permute-start | bytes 2168 | tf_op jit(solution)/shard_map/ppermute | solution.py:23
  407.6 5.5 %collective-permute-done.91 = f32[2,1,16,128]{3,2,1,0:T(8,128)S(1)} collective-permute-done((f32[2,1,16,128]{3,2,1,0:T(8,128)S(1)}, f32[2,1,16,128]{3,2,1,0:T(8,128)S(1)}, u32[]{:S(2)}, u32[]{:S(2)}) %collective-permute-start.91) | collective-permute-done | bytes 16416 | tf_op jit(solution)/shard_map/ppermute | solution.py:24
  439.0 10.8 %all-reduce.1 = f32[8,16]{0,1:T(8,128)S(1)} all-reduce(f32[8,16]{0,1:T(8,128)S(1)} %copy.1047), channel_id=2, replica_groups=mesh['gx'=4,'gy'=2,'gz'=4] {'gz'}, use_global_device_ids=true, to_apply=%region_10.11.clone | all-reduce | flops 128 | bytes 1024
  (769 shorter events, 323.6 us)
Async XLA Ops:
  37.2 14.5 %collective-permute-start.10 = (f32[10,18,1]{2,1,0:T(8,128)S(1)}, f32[10,18,1]{2,1,0:T(8,128)S(1)}, u32[]{:S(2)}, u32[]{:S(2)}) collective-permute-start(f32[10,18,1]{2,1,0:T(8,128)S(1)} %get-tuple-element.532), channel_id=1, source_target_pairs={{1,0},{2,1},{3,2},{5,4},{6,5},{7,6},{9,8},{10,9},{11,10},{13,12},{... | collective-permute-start | bytes 2168 | tf_op jit(solution)/shard_map/ppermute | solution.py:24
  38.5 13.2 %collective-permute-start.11 = (f32[10,18,1]{2,1,0:T(8,128)S(1)}, f32[10,18,1]{2,1,0:T(8,128)S(1)}, u32[]{:S(2)}, u32[]{:S(2)}) collective-permute-start(f32[10,18,1]{2,1,0:T(8,128)S(1)} %get-tuple-element.533), channel_id=1, source_target_pairs={{0,1},{1,2},{2,3},{4,5},{5,6},{6,7},{8,9},{9,10},{10,11},{12,13},{... | collective-permute-start | bytes 2168 | tf_op jit(solution)/shard_map/ppermute | solution.py:23
  58.0 13.5 %collective-permute-start.14 = (f32[10,1,128]{2,1,0:T(1,128)S(1)}, f32[10,1,128]{2,1,0:T(1,128)S(1)}, u32[]{:S(2)}, u32[]{:S(2)}) collective-permute-start(f32[10,1,128]{2,1,0:T(1,128)S(1)} %get-tuple-element.545), channel_id=1, source_target_pairs={{4,0},{5,1},{6,2},{7,3},{12,8},{13,9},{14,10},{15,11},{20,16},{21,... | collective-permute-start | bytes 15368 | tf_op jit(solution)/shard_map/ppermute | solution.py:24
  59.3 12.2 %collective-permute-start.15 = (f32[10,1,128]{2,1,0:T(1,128)S(1)}, f32[10,1,128]{2,1,0:T(1,128)S(1)}, u32[]{:S(2)}, u32[]{:S(2)}) collective-permute-start(f32[10,1,128]{2,1,0:T(1,128)S(1)} %get-tuple-element.544), channel_id=1, source_target_pairs={{0,4},{1,5},{2,6},{3,7},{8,12},{9,13},{10,14},{11,15},{16,20},{17,... | collective-permute-start | bytes 15368 | tf_op jit(solution)/shard_map/ppermute | solution.py:23
  63.8 22.0 %collective-permute-start.24 = (f32[1,8,64]{2,1,0:T(8,128)S(1)}, f32[1,8,64]{2,1,0:T(8,128)S(1)}, u32[]{:S(2)}, u32[]{:S(2)}) collective-permute-start(f32[1,8,64]{2,1,0:T(8,128)S(1)} %get-tuple-element.608), channel_id=1, source_target_pairs={{8,0},{16,8},{24,16},{9,1},{17,9},{25,17},{10,2},{18,10},{26,18},{... | collective-permute-start | bytes 6152 | tf_op jit(solution)/shard_map/ppermute | solution.py:24
  65.1 20.8 %collective-permute-start.25 = (f32[1,8,64]{2,1,0:T(8,128)S(1)}, f32[1,8,64]{2,1,0:T(8,128)S(1)}, u32[]{:S(2)}, u32[]{:S(2)}) collective-permute-start(f32[1,8,64]{2,1,0:T(8,128)S(1)} %get-tuple-element.607), channel_id=1, source_target_pairs={{0,8},{8,16},{16,24},{1,9},{9,17},{17,25},{2,10},{10,18},{18,26},{... | collective-permute-start | bytes 6152 | tf_op jit(solution)/shard_map/ppermute | solution.py:23
  80.0 11.7 %collective-permute-start.18 = (f32[1,16,128]{2,1,0:T(8,128)S(1)}, f32[1,16,128]{2,1,0:T(8,128)S(1)}, u32[]{:S(2)}, u32[]{:S(2)}) collective-permute-start(f32[1,16,128]{2,1,0:T(8,128)S(1)} %get-tuple-element.557), channel_id=1, source_target_pairs={{8,0},{16,8},{24,16},{9,1},{17,9},{25,17},{10,2},{18,10},{26,18},{... | collective-permute-start | bytes 24584 | tf_op jit(solution)/shard_map/ppermute | solution.py:24
  81.3 10.4 %collective-permute-start.19 = (f32[1,16,128]{2,1,0:T(8,128)S(1)}, f32[1,16,128]{2,1,0:T(8,128)S(1)}, u32[]{:S(2)}, u32[]{:S(2)}) collective-permute-start(f32[1,16,128]{2,1,0:T(8,128)S(1)} %get-tuple-element.556), channel_id=1, source_target_pairs={{0,8},{8,16},{16,24},{1,9},{9,17},{17,25},{2,10},{10,18},{18,26},{... | collective-permute-start | bytes 24584 | tf_op jit(solution)/shard_map/ppermute | solution.py:23
  85.9 11.7 %collective-permute-start.26 = (f32[6,1,64]{2,1,0:T(1,128)S(1)}, f32[6,1,64]{2,1,0:T(1,128)S(1)}, u32[]{:S(2)}, u32[]{:S(2)}) collective-permute-start(f32[6,1,64]{2,1,0:T(1,128)S(1)} %get-tuple-element.594), channel_id=1, source_target_pairs={{4,0},{5,1},{6,2},{7,3},{12,8},{13,9},{14,10},{15,11},{20,16},{21,... | collective-permute-start | bytes 4616 | tf_op jit(solution)/shard_map/ppermute | solution.py:24
  87.2 10.5 %collective-permute-start.27 = (f32[6,1,64]{2,1,0:T(1,128)S(1)}, f32[6,1,64]{2,1,0:T(1,128)S(1)}, u32[]{:S(2)}, u32[]{:S(2)}) collective-permute-start(f32[6,1,64]{2,1,0:T(1,128)S(1)} %get-tuple-element.593), channel_id=1, source_target_pairs={{0,4},{1,5},{2,6},{3,7},{8,12},{9,13},{10,14},{11,15},{16,20},{17,... | collective-permute-start | bytes 4616 | tf_op jit(solution)/shard_map/ppermute | solution.py:23
  99.1 11.9 %collective-permute-start.22 = (f32[10,18,1]{2,1,0:T(8,128)S(1)}, f32[10,18,1]{2,1,0:T(8,128)S(1)}, u32[]{:S(2)}, u32[]{:S(2)}) collective-permute-start(f32[10,18,1]{2,1,0:T(8,128)S(1)} %get-tuple-element.528), channel_id=1, source_target_pairs={{1,0},{2,1},{3,2},{5,4},{6,5},{7,6},{9,8},{10,9},{11,10},{13,12},{... | collective-permute-start | bytes 2168 | tf_op jit(solution)/shard_map/ppermute | solution.py:24
  100.4 10.6 %collective-permute-start.23 = (f32[10,18,1]{2,1,0:T(8,128)S(1)}, f32[10,18,1]{2,1,0:T(8,128)S(1)}, u32[]{:S(2)}, u32[]{:S(2)}) collective-permute-start(f32[10,18,1]{2,1,0:T(8,128)S(1)} %get-tuple-element.529), channel_id=1, source_target_pairs={{0,1},{1,2},{2,3},{4,5},{5,6},{6,7},{8,9},{9,10},{10,11},{12,13},{... | collective-permute-start | bytes 2168 | tf_op jit(solution)/shard_map/ppermute | solution.py:23
  105.2 14.1 %collective-permute-start.28 = (f32[6,10,1]{2,1,0:T(8,128)S(1)}, f32[6,10,1]{2,1,0:T(8,128)S(1)}, u32[]{:S(2)}, u32[]{:S(2)}) collective-permute-start(f32[6,10,1]{2,1,0:T(8,128)S(1)} %get-tuple-element.580), channel_id=1, source_target_pairs={{1,0},{2,1},{3,2},{5,4},{6,5},{7,6},{9,8},{10,9},{11,10},{13,12},{... | collective-permute-start | bytes 728 | tf_op jit(solution)/shard_map/ppermute | solution.py:24
  106.5 12.8 %collective-permute-start.29 = (f32[6,10,1]{2,1,0:T(8,128)S(1)}, f32[6,10,1]{2,1,0:T(8,128)S(1)}, u32[]{:S(2)}, u32[]{:S(2)}) collective-permute-start(f32[6,10,1]{2,1,0:T(8,128)S(1)} %get-tuple-element.579), channel_id=1, source_target_pairs={{0,1},{1,2},{2,3},{4,5},{5,6},{6,7},{8,9},{9,10},{10,11},{12,13},{... | collective-permute-start | bytes 728 | tf_op jit(solution)/shard_map/ppermute | solution.py:23
  119.4 10.4 %collective-permute-start.30 = (f32[1,8,64]{2,1,0:T(8,128)S(1)}, f32[1,8,64]{2,1,0:T(8,128)S(1)}, u32[]{:S(2)}, u32[]{:S(2)}) collective-permute-start(f32[1,8,64]{2,1,0:T(8,128)S(1)} %get-tuple-element.606), channel_id=1, source_target_pairs={{8,0},{16,8},{24,16},{9,1},{17,9},{25,17},{10,2},{18,10},{26,18},{... | collective-permute-start | bytes 6152 | tf_op jit(solution)/shard_map/ppermute | solution.py:24
  123.8 26.3 %collective-permute-start.48 = (f32[1,4,32]{2,1,0:T(4,128)S(1)}, f32[1,4,32]{2,1,0:T(4,128)S(1)}, u32[]{:S(2)}, u32[]{:S(2)}) collective-permute-start(f32[1,4,32]{2,1,0:T(4,128)S(1)} %get-tuple-element.618), channel_id=1, source_target_pairs={{8,0},{16,8},{24,16},{9,1},{17,9},{25,17},{10,2},{18,10},{26,18},{... | collective-permute-start | bytes 1544 | tf_op jit(solution)/shard_map/ppermute | solution.py:24
  125.0 25.0 %collective-permute-start.49 = (f32[1,4,32]{2,1,0:T(4,128)S(1)}, f32[1,4,32]{2,1,0:T(4,128)S(1)}, u32[]{:S(2)}, u32[]{:S(2)}) collective-permute-start(f32[1,4,32]{2,1,0:T(4,128)S(1)} %get-tuple-element.617), channel_id=1, source_target_pairs={{0,8},{8,16},{16,24},{1,9},{9,17},{17,25},{2,10},{10,18},{18,26},{... | collective-permute-start | bytes 1544 | tf_op jit(solution)/shard_map/ppermute | solution.py:23
  167.7 10.7 %collective-permute-start.42 = (f32[1,8,64]{2,1,0:T(8,128)S(1)}, f32[1,8,64]{2,1,0:T(8,128)S(1)}, u32[]{:S(2)}, u32[]{:S(2)}) collective-permute-start(f32[1,8,64]{2,1,0:T(8,128)S(1)} %get-tuple-element.602), channel_id=1, source_target_pairs={{8,0},{16,8},{24,16},{9,1},{17,9},{25,17},{10,2},{18,10},{26,18},{... | collective-permute-start | bytes 6152 | tf_op jit(solution)/shard_map/ppermute | solution.py:24
  169.0 9.4 %collective-permute-start.43 = (f32[1,8,64]{2,1,0:T(8,128)S(1)}, f32[1,8,64]{2,1,0:T(8,128)S(1)}, u32[]{:S(2)}, u32[]{:S(2)}) collective-permute-start(f32[1,8,64]{2,1,0:T(8,128)S(1)} %get-tuple-element.601), channel_id=1, source_target_pairs={{0,8},{8,16},{16,24},{1,9},{9,17},{17,25},{2,10},{10,18},{18,26},{... | collective-permute-start | bytes 6152 | tf_op jit(solution)/shard_map/ppermute | solution.py:23
  172.1 12.2 %collective-permute-start.52 = (f32[4,6,1]{2,0,1:T(4,128)S(1)}, f32[4,6,1]{2,0,1:T(4,128)S(1)}, u32[]{:S(2)}, u32[]{:S(2)}) collective-permute-start(f32[4,6,1]{2,0,1:T(4,128)S(1)} %get-tuple-element.611), channel_id=1, source_target_pairs={{1,0},{2,1},{3,2},{5,4},{6,5},{7,6},{9,8},{10,9},{11,10},{13,12},{... | collective-permute-start | bytes 296 | tf_op jit(solution)/shard_map/ppermute | solution.py:24
  173.4 10.9 %collective-permute-start.53 = (f32[4,6,1]{2,0,1:T(4,128)S(1)}, f32[4,6,1]{2,0,1:T(4,128)S(1)}, u32[]{:S(2)}, u32[]{:S(2)}) collective-permute-start(f32[4,6,1]{2,0,1:T(4,128)S(1)} %get-tuple-element.612), channel_id=1, source_target_pairs={{0,1},{1,2},{2,3},{4,5},{5,6},{6,7},{8,9},{9,10},{10,11},{12,13},{... | collective-permute-start | bytes 296 | tf_op jit(solution)/shard_map/ppermute | solution.py:23
  194.9 12.5 %all-to-all-start = ((f32[4,1,768]{2,1,0:T(1,128)}), f32[4,1,768]{2,1,0:T(1,128)S(1)}, u32[]{:S(2)}, u32[]{:S(2)}) async-start(f32[4,1,768]{2,1,0:T(1,128)} %reshape.619), calls=%async_computation | async-start | bytes 24576 | tf_op jit(solution)/shard_map/all_to_all | solution.py:127
  423.1 10.6 %collective-permute-start.94 = (f32[2,10,18,1]{3,2,1,0:T(8,128)S(1)}, f32[2,10,18,1]{3,2,1,0:T(8,128)S(1)}, u32[]{:S(2)}, u32[]{:S(2)}) collective-permute-start(f32[2,10,18,1]{3,2,1,0:T(8,128)S(1)} %get-tuple-element.512), channel_id=1, source_target_pairs={{0,1},{1,2},{2,3},{4,5},{5,6},{6,7},{8,9},{9,10},{10,11},{12,13},{... | collective-permute-start | bytes 4328 | tf_op jit(solution)/shard_map/ppermute | solution.py:23
  427.5 10.7 %collective-permute-start.95 = (f32[2,10,18,1]{3,2,1,0:T(8,128)S(1)}, f32[2,10,18,1]{3,2,1,0:T(8,128)S(1)}, u32[]{:S(2)}, u32[]{:S(2)}) collective-permute-start(f32[2,10,18,1]{3,2,1,0:T(8,128)S(1)} %get-tuple-element.513), channel_id=1, source_target_pairs={{1,0},{2,1},{3,2},{5,4},{6,5},{7,6},{9,8},{10,9},{11,10},{13,12},{... | collective-permute-start | bytes 4328 | tf_op jit(solution)/shard_map/ppermute | solution.py:24
  (78 other events, 693.9 us)
where the time goes:
time: 453 us; the launch traced here: 450 us
  starting transfers between devices  277 us (61%)
  waiting for transfers between devices  67.7 us (15%)
  local copies, waits for them, and re-layouts  66.1 us (15%)
  blocking collectives  18.7 us (4%)
  other arithmetic  15.7 us (3%)
  between operations  4.58 us (1%)
    ppermute x48, starting transfers between devices, padded_2(): before = lax.ppermute(last, axis, up)  208 us
    ppermute x48, starting transfers between devices, padded_2(): after = lax.ppermute(first, axis, down)  62 us
    ppermute x48, waiting for transfers between devices, padded_2(): before = lax.ppermute(last, axis, up)  41.2 us
    broadcast_in_dim x382, local copies, waits for them, and re-layouts, line_solve(): solved = lax.linalg.tridiagonal_solve(-lower, total, -upper, rhs[..., None])  37.4 us
    ppermute x48, waiting for transfers between devices, padded_2(): after = lax.ppermute(first, axis, down)  21.1 us
    reshape x3, local copies, waits for them, and re-layouts, restrict(): field.reshape(shape[0] // 2, 2, shape[1] // 2, 2, shape[2] // 2, 2)  11.5 us
    unnamed x1, blocking collectives  10.8 us
  transfers between devices with their start and end apart: 97, of which 48 were waited for; matrix products, arithmetic and copies ran while one was open for 4% of the time, Pallas kernels for 0%

commit v1 on v0

v1 whole, which is shorter than its diff:
```python
import functools
import math

import jax
import jax.numpy as jnp
from jax import lax
from jax.experimental import pallas as pl
from jax.experimental.pallas import tpu as pltpu
from jax.sharding import PartitionSpec as P

ANISO = 200.0
OMEGA = 0.8
HALO = 10
SEND = 16
MESH = pl.DeviceIdType.MESH
F32 = jnp.float32


def kernel(
    n_x, n_y, n_z, cx_len, cy_len, cz_len, n_total,
    source_ref, state_ref, logc_ref, lat_ref, owners_ref,
    adj_ref, grad_ref,
    gath, sgath, stage_lo, stage_hi, sstage_lo, sstage_hi,
    c0, x0, y0, z0, d0, i0, b0, va, vb,
    c1, x1, y1, z1, d1, i1, b1, ma, mb,
    c2, z2, d2, r2, im2, spike,
    s0, iface, sides, mid_lo, mid_hi, spk_lo, spk_hi, part,
    main_send, main_recv, lo_send, lo_recv, hi_send, hi_recv,
    st_send, st_recv, stz_send, stz_recv,
    mid_send, mid_recv, if_send, if_recv, pt_send, pt_recv,
):
    nd = n_x * n_y
    lanes = cx_len * cy_len
    gx, gy, gz = lax.axis_index("gx"), lax.axis_index("gy"), lax.axis_index("gz")
    me = gx * n_y + gy
    up, down = lax.rem(gz + 1, n_z), lax.rem(gz + n_z - 1, n_z)
    Z0, Z1, Z2 = cz_len + 2 * HALO, cz_len // 2 + HALO, cz_len // 4 + 2
    H1 = HALO // 2
    L1, L2 = cz_len // 2, cz_len // 4

    def place(k, z):
        peer = lax.rem(me + k, nd)
        return (lax.div(peer, n_y), lax.rem(peer, n_y), z)

    barrier = pltpu.get_barrier_semaphore()
    greeted = [place(k, gz) for k in range(1, nd)]
    greeted += [place(k, z) for z in (up, down) for k in range(nd)]
    greeted += [(gx, gy, lax.rem(gz + j, n_z)) for j in range(2, n_z - 1)]
    for device in greeted:
        pl.semaphore_signal(barrier, inc=1, device_id=device, device_id_type=MESH)

    lane = lax.broadcasted_iota(jnp.int32, (nd, lanes), 1)
    sub = lax.broadcasted_iota(jnp.int32, (nd, lanes), 0)
    xs, ys = lane // cy_len, lane % cy_len
    dx, dy = sub // n_y, sub % n_y
    lane8 = lax.broadcasted_iota(jnp.int32, (cx_len, lanes), 1)
    row8 = lax.broadcasted_iota(jnp.int32, (cx_len, lanes), 0)
    lat = jnp.zeros((cx_len, lanes), F32)
    for y in range(cy_len):
        lat = jnp.where(lane8 % cy_len == y, lat_ref[:, y : y + 1], lat)
    lat = jnp.sum(jnp.where(lane8 // cy_len == row8, lat, 0.0), axis=0, keepdims=True)

    def rows_of(ref):
        return ref[...].reshape(lanes, cz_len).T

    coef = jnp.exp(rows_of(logc_ref) + lat)
    src = rows_of(source_ref)
    state = rows_of(state_ref)
    gath[me, 0:cz_len, :] = coef
    gath[me, cz_len : 2 * cz_len, :] = src
    line = owners_ref[0]
    for j in range(16):
        if 0 < j < n_z:
            same = jnp.broadcast_to(line[:, j : j + 1], (1, lanes)) == jnp.broadcast_to(
                line[:, j - 1 : j], (1, lanes)
            )
            gath[me, 2 * cz_len + j : 2 * cz_len + j + 1, :] = jnp.where(same, 1.0, 0.0)
        else:
            gath[me, 2 * cz_len + j : 2 * cz_len + j + 1, :] = jnp.zeros((1, lanes), F32)
    stage_lo[0:SEND, :] = coef[cz_len - SEND :]
    stage_lo[SEND : 2 * SEND, :] = src[cz_len - SEND :]
    stage_hi[0:SEND, :] = coef[:SEND]
    stage_hi[SEND : 2 * SEND, :] = src[:SEND]
    sgath[me, 0:cz_len, :] = state
    sstage_lo[...] = state[cz_len - 8 :]
    sstage_hi[...] = state[:8]
    pl.semaphore_wait(barrier, len(greeted))

    base_lo = 2 * cz_len + 16
    base_hi = base_lo + 2 * SEND
    sent = []

    def copy(src_at, dst_at, ssem, rsem, device):
        c = pltpu.make_async_remote_copy(
            src_ref=src_at, dst_ref=dst_at, send_sem=ssem, recv_sem=rsem,
            device_id=device, device_id_type=MESH,
        )
        c.start()
        return c

    main, los, his = [], [], []
    for k in range(1, nd):
        body = gath.at[me, pl.ds(0, base_lo)]
        main.append(copy(body, body, main_send.at[k], main_recv.at[k], place(k, gz)))
    for k in range(nd):
        los.append(copy(stage_lo, gath.at[me, pl.ds(base_lo, 2 * SEND)],
                        lo_send.at[k], lo_recv.at[k], place(k, up)))
        his.append(copy(stage_hi, gath.at[me, pl.ds(base_hi, 2 * SEND)],
                        hi_send.at[k], hi_recv.at[k], place(k, down)))

    def roll(v, shift, axis):
        return pltpu.roll(v, shift % v.shape[axis], axis)

    def masks(s):
        return dict(
            s=s,
            xhi=(xs >= cx_len - s)[None], xlo=(xs < s)[None],
            yhi=(ys >= cy_len - s)[None], ylo=(ys < s)[None],
            xin=jnp.where((xs >= cx_len - s) & (dx == n_x - 1), 0.0, 0.5)[None],
            yin=jnp.where((ys >= cy_len - s) & (dy == n_y - 1), 0.0, 0.5)[None],
            edge=(
                jnp.where((xs >= cx_len - s) & (dx == n_x - 1), 1.0, 0.0)
                + jnp.where((xs < s) & (dx == 0), 1.0, 0.0)
                + jnp.where((ys >= cy_len - s) & (dy == n_y - 1), 1.0, 0.0)
                + jnp.where((ys < s) & (dy == 0), 1.0, 0.0)
            )[None],
            xbit=(xs // s % 2 == 0)[None], ybit=(ys // s % 2 == 0)[None],
        )

    def pick(mask, a, b):
        return jnp.where(jnp.broadcast_to(mask, a.shape), a, b)

    def x_next(v, m):
        r = roll(v, -m["s"] * cy_len, 2)
        return pick(m["xhi"], roll(r, -n_y, 1), r)

    def x_prev(v, m):
        r = roll(v, m["s"] * cy_len, 2)
        return pick(m["xlo"], roll(r, n_y, 1), r)

    def y_next(v, m):
        r = roll(v, -m["s"], 2)
        return pick(m["yhi"], roll(roll(v, -1, 1), cy_len - m["s"], 2), r)

    def y_prev(v, m):
        r = roll(v, m["s"], 2)
        return pick(m["ylo"], roll(roll(v, 1, 1), m["s"] - cy_len, 2), r)

    def block_mean(pair, m):
        s = m["s"]
        v = pair + pick(m["ybit"], roll(pair, -s, 2), roll(pair, s, 2))
        w = s * cy_len
        v = v + pick(m["xbit"], roll(v, -w, 2), roll(v, w, 2))
        return 0.125 * v

    m0, m1, m2 = masks(1), masks(2), masks(4)
    first_dev, last_dev = gz == 0, gz == n_z - 1
    zero_plane = jnp.zeros((1, nd, lanes), F32)

    def loop(count, step, body):
        def run(i, carry):
            body(i * step)
            return carry
        lax.fori_loop(0, count // step, run, 0)

    def pads(ref):
        ref[0:1] = zero_plane
        ref[ref.shape[0] - 1 :] = zero_plane

    for ref in (c0, va, vb, c1, ma, mb, c2):
        pads(ref)

    def level(c, length, halo, own, scale, m, xr, yr, zr, dr, ir):
        za = scale * ANISO
        zr[length : length + 1] = zero_plane

        def body(i):
            k = i
            here = c[pl.ds(k + 1, 1)]
            below, above = c[pl.ds(k, 1)], c[pl.ds(k + 2, 1)]
            cut_lo = (k == 0) | (first_dev & (k == halo)) | (last_dev & (k == halo + own))
            cut_hi = (k == length - 1) | (first_dev & (k == halo - 1)) | (
                last_dev & (k == halo + own - 1))
            keep_lo = jnp.where(cut_lo, 0.0, 0.5 * za)
            keep_hi = jnp.where(cut_hi, 0.0, 0.5 * za)
            edge_z = jnp.where(cut_lo, za, 0.0) + jnp.where(cut_hi, za, 0.0)
            wz = keep_lo * (below + here)
            zr[pl.ds(k, 1)] = wz
            wx = (scale * m["xin"]) * (here + x_next(here, m))
            wy = (scale * m["yin"]) * (here + y_next(here, m))
            diag = wx + x_prev(wx, m) + wy + y_prev(wy, m) + (scale * m["edge"]) * here
            diag = diag + wz + keep_hi * (above + here) + edge_z * here
            dr[pl.ds(k, 1)] = diag
            if xr is not None:
                xr[pl.ds(k, 1)] = wx
                yr[pl.ds(k, 1)] = wy
                ir[pl.ds(k, 1)] = OMEGA / diag

        loop(length, 1, body)

    def pull(v, k, step, m, xr, yr, zr):
        here = v[pl.ds(k + 1, step)]
        wx, wy = xr[pl.ds(k, step)], yr[pl.ds(k, step)]
        total = zr[pl.ds(k, step)] * v[pl.ds(k, step)]
        total = total + zr[pl.ds(k + 1, step)] * v[pl.ds(k + 2, step)]
        total = total + (wx * x_next(here, m) + x_prev(wx * here, m))
        total = total + (wy * y_next(here, m) + y_prev(wy * here, m))
        return here, total

    def sweep(v, out, b, start, stop, m, xr, yr, zr, ir, step=4):
        def body(i):
            k = start + i
            here, total = pull(v, k, step, m, xr, yr, zr)
            out[pl.ds(k + 1, step)] = (1.0 - OMEGA) * here + ir[pl.ds(k, step)] * (
                b[pl.ds(k, step)] + total)
        loop(stop - start, step, body)

    fine = (m0, x0, y0, z0)
    mid = (m1, x1, y1, z1)

    for c in main:
        c.wait()
    for c in los + his:
        c.wait()
    flat = gath.reshape(nd * gath.shape[1], lanes)
    sflat = sgath.reshape(nd * sgath.shape[1], lanes)

    def plane(row):
        return flat[pl.ds(row, nd, stride=gath.shape[1]), :][None]

    def spread(i):
        c0[pl.ds(1 + HALO + i, 1)] = plane(i)
        b0[pl.ds(HALO + i, 1)] = plane(cz_len + i)

    loop(cz_len, 1, spread)

    def spread_halo(i):
        c0[pl.ds(1 + i, 1)] = plane(base_lo + SEND - HALO + i)
        b0[pl.ds(i, 1)] = plane(base_lo + 2 * SEND - HALO + i)
        c0[pl.ds(1 + HALO + cz_len + i, 1)] = plane(base_hi + i)
        b0[pl.ds(HALO + cz_len + i, 1)] = plane(base_hi + SEND + i)

    loop(HALO, 1, spread_halo)

    states = []
    for k in range(1, nd):
        body = sgath.at[me, pl.ds(0, cz_len)]
        states.append(copy(body, body, st_send.at[k], st_recv.at[k], place(k, gz)))
    states.append(copy(sstage_lo, sgath.at[me, pl.ds(cz_len, 8)],
                       stz_send.at[0], stz_recv.at[0], (gx, gy, up)))
    states.append(copy(sstage_hi, sgath.at[me, pl.ds(cz_len + 8, 8)],
                       stz_send.at[1], stz_recv.at[1], (gx, gy, down)))

    def pairs(ref, k, step):
        v = ref[pl.ds(k, 2 * step)].reshape(step, 2, nd, lanes)
        return v[:, 0] + v[:, 1]

    def coarsen1(K):
        c1[pl.ds(K + 1, 2)] = block_mean(pairs(c0, 1 + 2 * K, 2), m0)

    loop(Z1, 2, coarsen1)

    def coarsen2(K):
        c2[pl.ds(K + 1, 2)] = block_mean(pairs(c1, 1 + H1 - 2 + 2 * K, 2), m1)

    loop(Z2, 2, coarsen2)
    level(c0, Z0, HALO, cz_len, 1.0, m0, x0, y0, z0, d0, i0)
    level(c1, Z1, H1, L1, 0.25, m1, x1, y1, z1, d1, i1)
    level(c2, Z2, 1, L2, 0.0625, m2, None, None, z2, d2, None)

    def first0(k):
        va[pl.ds(k + 1, 4)] = i0[pl.ds(k, 4)] * b0[pl.ds(k, 4)]

    loop(Z0, 4, first0)
    sweep(va, vb, b0, 2, Z0 - 2, *fine, i0)
    sweep(vb, va, b0, 2, Z0 - 2, *fine, i0)

    def resid0_all():
        def body(i):
            K = 2 + i
            k = 2 * K
            here, total = pull(va, k, 4, *fine)
            r = b0[pl.ds(k, 4)] + total - d0[pl.ds(k, 4)] * here
            r = r.reshape(2, 2, nd, lanes)
            b1[pl.ds(K, 2)] = block_mean(r[:, 0] + r[:, 1], m0)
        loop(Z1 - 4, 2, body)

    resid0_all()

    def first1(i):
        k = 2 + i
        ma[pl.ds(k + 1, 2)] = i1[pl.ds(k, 2)] * b1[pl.ds(k, 2)]

    loop(Z1 - 4, 2, first1)
    sweep(ma, mb, b1, 3, Z1 - 3, *mid, i1)
    sweep(mb, ma, b1, 3, Z1 - 3, *mid, i1)

    mids = [
        copy(ma.at[pl.ds(1 + L1, H1)], mid_lo.at[0], mid_send.at[0], mid_recv.at[0], (gx, gy, up)),
        copy(b1.at[pl.ds(L1, H1)], mid_lo.at[1], mid_send.at[1], mid_recv.at[1], (gx, gy, up)),
        copy(ma.at[pl.ds(1 + H1, H1)], mid_hi.at[0], mid_send.at[2], mid_recv.at[2], (gx, gy, down)),
        copy(b1.at[pl.ds(H1, H1)], mid_hi.at[1], mid_send.at[3], mid_recv.at[3], (gx, gy, down)),
    ]

    def resid1(K):
        k = H1 + 2 * K
        here, total = pull(ma, k, 4, *mid)
        r = b1[pl.ds(k, 4)] + total - d1[pl.ds(k, 4)] * here
        r = r.reshape(2, 2, nd, lanes)
        r2[pl.ds(K, 2)] = block_mean(r[:, 0] + r[:, 1], m1)

    loop(L2, 2, resid1)

    inv = 1.0 / d2[1]
    y_now, p_now = r2[0], jnp.ones((nd, lanes), F32)
    im2[0], spike[0, 0], spike[1, 0] = inv, y_now, p_now

    def forward(k, carry):
        inv, y_now, p_now = carry
        e = z2[k + 1]
        t = e * inv
        inv = 1.0 / (d2[k + 1] - e * t)
        y_now = r2[k] + t * y_now
        p_now = t * p_now
        im2[k], spike[0, k], spike[1, k] = inv, y_now, p_now
        return inv, y_now, p_now

    inv, y_now, p_now = lax.fori_loop(1, L2, forward, (inv, y_now, p_now))
    last = (y_now * inv, p_now * inv, inv)
    for i in range(3):
        spike[i, L2 - 1] = last[i]

    def backward(i, carry):
        g, p, q = carry
        k = L2 - 2 - i
        e, inv = z2[k + 2], im2[k]
        g = inv * (spike[0, k] + e * g)
        p = inv * (spike[1, k] + e * p)
        q = inv * (e * q)
        spike[0, k], spike[1, k], spike[2, k] = g, p, q
        return g, p, q

    head = lax.fori_loop(0, L2 - 1, backward, last)
    for i in range(3):
        iface[gz, i] = head[i]
        iface[gz, 3 + i] = last[i]
    iface[gz, 6] = z2[1] * flat[pl.ds(2 * cz_len + gz, nd, stride=gath.shape[1]), :]
    ifs = []
    for j in range(1, n_z):
        ifs.append(copy(iface.at[gz], iface.at[gz], if_send.at[j], if_recv.at[j],
                        (gx, gy, lax.rem(gz + j, n_z))))
    ifs.append(copy(spike.at[:, pl.ds(L2 - 3, 3)], spk_lo, if_send.at[n_z], if_recv.at[n_z],
                    (gx, gy, up)))
    ifs.append(copy(spike.at[:, pl.ds(0, 3)], spk_hi, if_send.at[n_z + 1], if_recv.at[n_z + 1],
                    (gx, gy, down)))

    for c in states:
        c.wait()

    def splane(row):
        return sflat[pl.ds(row, nd, stride=sgath.shape[1]), :][None]

    def spread_state(i):
        s0[pl.ds(1 + i, 1)] = splane(i)

    loop(cz_len, 1, spread_state)
    s0[0:1] = jnp.where(first_dev, 0.0, splane(cz_len + 7))
    s0[cz_len + 1 :] = jnp.where(last_dev, 0.0, splane(cz_len + 8))

    for c in mids + ifs:
        c.wait()

    zero = jnp.zeros((nd, lanes), F32)
    A, B = zero, zero
    kept = []
    for j in range(n_z):
        c = iface[j, 6]
        g, p, q = iface[j, 0], iface[j, 1], iface[j, 2]
        gl, plast, ql = iface[j, 3], iface[j, 4], iface[j, 5]
        inv = 1.0 / (1.0 - p * c * B)
        F = (g + p * c * A) * inv
        G = q * inv
        kept.append((c, A, B, F, G))
        nxt = iface[j + 1, 6] if j + 1 < n_z else zero
        tail = plast * c
        A, B = gl + tail * (A + B * F), (ql + tail * B * G) * nxt
    right = zero
    for j in reversed(range(n_z)):
        c, A, B, F, G = kept[j]
        head = F + G * right
        sides[j, 0] = c * (A + B * head)
        sides[j, 1] = right
        right = c * head

    L, R = sides[gz, 0], sides[gz, 1]

    def twice(v):
        return jnp.broadcast_to(v[:, None], (v.shape[0], 2, nd, lanes)).reshape(
            2 * v.shape[0], nd, lanes)

    def correct(K):
        x = spike[0, pl.ds(K, 2)] + spike[1, pl.ds(K, 2)] * L + spike[2, pl.ds(K, 2)] * R
        k = 1 + H1 + 2 * K
        ma[pl.ds(k, 4)] = ma[pl.ds(k, 4)] + twice(x)

    loop(L2, 2, correct)
    xl = spk_lo[0] + spk_lo[1] * sides[down, 0] + spk_lo[2] * sides[down, 1]
    ma[1 : 1 + H1] = mid_lo[0] + twice(xl)[6 - H1 :]
    b1[0:H1] = mid_lo[1]
    xh = spk_hi[0] + spk_hi[1] * sides[up, 0] + spk_hi[2] * sides[up, 1]
    ma[1 + H1 + L1 : 1 + 2 * H1 + L1] = mid_hi[0] + twice(xh)[:H1]
    b1[H1 + L1 :] = mid_hi[1]

    sweep(ma, mb, b1, 1, Z1 - 1, *mid, i1)
    sweep(mb, ma, b1, 1, Z1 - 1, *mid, i1)
    sweep(ma, mb, b1, 3, Z1 - 3, *mid, i1)

    def raise0(i):
        K = 3 + i
        k = 1 + 2 * K
        va[pl.ds(k, 4)] = va[pl.ds(k, 4)] + twice(mb[pl.ds(K + 1, 2)])

    loop(Z1 - 6, 2, raise0)
    sweep(va, vb, b0, HALO - 4, HALO + cz_len + 4, *fine, i0)
    sweep(vb, va, b0, HALO - 2, HALO + cz_len + 2, *fine, i0)
    sweep(va, vb, b0, HALO - 2, HALO + cz_len + 2, *fine, i0)

    def terms(i, acc):
        a, s = vb[pl.ds(HALO + 1 + i, 1)], s0[pl.ds(1 + i, 1)]
        tx = m0["xin"] * ((a - x_next(a, m0)) * (s - x_next(s, m0)))
        ty = m0["yin"] * ((a - y_next(a, m0)) * (s - y_next(s, m0)))
        t = tx + x_prev(tx, m0) + ty + y_prev(ty, m0) + m0["edge"] * (a * s)
        lo = first_dev & (i == 0)
        hi = last_dev & (i == cz_len - 1)
        below, above = vb[pl.ds(HALO + i, 1)], vb[pl.ds(HALO + 2 + i, 1)]
        t = t + jnp.where(lo, a * s, 0.5 * ((a - below) * (s - s0[pl.ds(i, 1)])))
        t = t + jnp.where(hi, a * s, 0.5 * ((a - above) * (s - s0[pl.ds(2 + i, 1)])))
        return acc + (c0[pl.ds(HALO + 1 + i, 1)] * t)[0]

    acc = lax.fori_loop(0, cz_len, terms, zero)
    part[gz] = acc
    parts = []
    for j in range(1, n_z):
        parts.append(copy(part.at[gz], part.at[gz], pt_send.at[j], pt_recv.at[j],
                          (gx, gy, lax.rem(gz + j, n_z))))

    vflat = vb.reshape(vb.shape[0] * nd, lanes)
    own = vflat[pl.ds((HALO + 1) * nd + me, cz_len, stride=nd), :]
    adj_ref[...] = own.T.reshape(cx_len, cy_len, cz_len)

    for c in parts:
        c.wait()
    total = part[0]
    for j in range(1, n_z):
        total = total + part[j]
    row = jnp.sum(jnp.where(sub == me, total, 0.0), axis=0, keepdims=True)
    row = jnp.broadcast_to(row, (cx_len, lanes)) * (-1.0 / math.sqrt(n_total))
    width = cy_len // n_z
    for j in range(width):
        here = lane8 == row8 * cy_len + gz * width + j
        grad_ref[:, j : j + 1] = jnp.sum(jnp.where(here, row, 0.0), axis=1, keepdims=True)


def solution(mesh):
    n_x, n_y, n_z = mesh.shape["gx"], mesh.shape["gy"], mesh.shape["gz"]
    nd = n_x * n_y

    def per_device(source, state, log_coef, lateral, owners):
        cx, cy, cz = source.shape
        lanes = cx * cy
        Z0, Z1, Z2, H1 = cz + 2 * HALO, cz // 2 + HALO, cz // 4 + 2, HALO // 2
        V = lambda *shape: pltpu.VMEM(shape, F32)
        pln = lambda k: V(k, nd, lanes)
        D = lambda k: pltpu.SemaphoreType.DMA((k,))
        vm = pl.BlockSpec(memory_space=pltpu.VMEM)
        return pl.pallas_call(
            functools.partial(kernel, n_x, n_y, n_z, cx, cy, cz, cz * n_z),
            out_shape=(
                jax.ShapeDtypeStruct((cx, cy, cz), F32),
                jax.ShapeDtypeStruct((cx, cy // n_z), F32),
            ),
            in_specs=[vm] * 5,
            out_specs=(vm, vm),
            scratch_shapes=[
                V(nd, 2 * cz + 16 + 4 * SEND, lanes), V(nd, cz + 16, lanes),
                V(2 * SEND, lanes), V(2 * SEND, lanes), V(8, lanes), V(8, lanes),
                pln(Z0 + 2), pln(Z0), pln(Z0), pln(Z0 + 1), pln(Z0), pln(Z0), pln(Z0),
                pln(Z0 + 2), pln(Z0 + 2),
                pln(Z1 + 2), pln(Z1), pln(Z1), pln(Z1 + 1), pln(Z1), pln(Z1), pln(Z1),
                pln(Z1 + 2), pln(Z1 + 2),
                pln(Z2 + 2), pln(Z2 + 1), pln(Z2), pln(cz // 4), pln(cz // 4),
                V(3, cz // 4, nd, lanes),
                pln(cz + 2), V(n_z, 7, nd, lanes), V(n_z, 2, nd, lanes),
                V(2, H1, nd, lanes), V(2, H1, nd, lanes),
                V(3, 3, nd, lanes), V(3, 3, nd, lanes), V(n_z, nd, lanes),
                D(nd), D(nd), D(nd), D(nd), D(nd), D(nd),
                D(nd), D(nd), D(2), D(2),
                D(4), D(4), D(n_z + 2), D(n_z + 2), D(n_z), D(n_z),
            ],
            compiler_params=pltpu.CompilerParams(
                collective_id=0, has_side_effects=True, vmem_limit_bytes=56 * 1024 * 1024
            ),
            cost_estimate=pl.CostEstimate(
                flops=100_000_000, bytes_accessed=400_000, transcendentals=20_000
            ),
        )(source, state, log_coef, lateral, owners)

    placed = (
        P("gx", "gy", "gz"),
        P("gx", "gy", "gz"),
        P("gx", "gy", "gz"),
        P("gx", "gy"),
        P("gx", "gy", None),
    )
    return jax.shard_map(
        per_device,
        mesh=mesh,
        in_specs=placed,
        out_specs=(P("gx", "gy", "gz"), P("gx", ("gy", "gz"))),
        check_vma=False,
    )
```

time: 453 us -> 147 us (0.32)
  starting transfers between devices: 277 us -> 0 us
  Pallas kernels: 0 us -> 143 us
  waiting for transfers between devices: 67.7 us -> 0 us
  local copies, waits for them, and re-layouts: 66.1 us -> 2.8 us
  blocking collectives: 18.7 us -> 0 us
  other arithmetic: 15.7 us -> 0 us
    ppermute x96 -> x0, starting transfers between devices: 270 us -> none  [the longest x48 208 us: padded_2(): before = lax.ppermute(last, axis, up)]
    pallas_call x0 -> x1, Pallas kernels: none -> 143 us  [per_device(): pl.pallas_call(functools.partial(kernel, n_x, n_y, n_z, cx, cy, cz, cz *...]
    ppermute x96 -> x0, waiting for transfers between devices: 62.3 us -> none  [the longest x48 41.2 us: padded_2(): before = lax.ppermute(last, axis, up)]
    broadcast_in_dim x384 -> x0, local copies, waits for them, and re-layouts: 40.1 us -> none  [the longest x382 37.4 us: line_solve(): solved = lax.linalg.tridiagonal_solve(-lower, total, -upper, rhs[..., None])]
    reshape x8 -> x0, local copies, waits for them, and re-layouts: 16.1 us -> none  [the longest x3 11.5 us: restrict(): field.reshape(shape[0] // 2, 2, shape[1] // 2, 2, shape[2] // 2, 2)]
    unnamed x1 -> x0, blocking collectives: 10.8 us -> none
    all_to_all x1 -> x0, blocking collectives: 7.91 us -> none  [per_device(): lax.all_to_all(solution.reshape(received.shape[1:]), 'gz', split_axis=2,...]
    all_to_all x1 -> x0, starting transfers between devices: 6.9 us -> none  [per_device(): lax.all_to_all(outgoing, 'gz', split_axis=3, concat_axis=3, tiled=True)]
  transfers between devices with their start and end apart: 97 -> 0, of which waited for: 48 -> 0; matrix products, arithmetic and copies ran while one was open for 4% -> 0% of each run, Pallas kernels for 0% -> 0%
where the time goes in v1:
time: 147 us
  Pallas kernels  143 us (97%)
  local copies, waits for them, and re-layouts  2.8 us (2%)
    pallas_call x1, Pallas kernels, per_device(): pl.pallas_call(functools.partial(kernel, n_x, n_y, n_z, cx, cy, cz, cz *...  143 us

profile of v1, /device:TPU:0, one launch (start us, length us, event | category | flops | bytes accessed | tf_op | source)
XLA Modules:
  0.0 146.6 jit_solution(86221359236728472)
XLA Ops:
  0.6 143.2 %shard_map.68 = (f32[8,16,128]{2,1,0:T(8,128)}, f32[8,4]{1,0:T(8,128)}) custom-call(f32[8,16,128]{2,1,0:T(8,128)} %source_ref.1, f32[8,16,128]{2,1,0:T(8,128)} %state_ref.1, f32[8,16,128]{2,1,0:T(8,128)} %logc_ref.1, f32[8,16]{1,0:T(8,128)} %lat_ref.1, s32[1,1,4]{2,1,0:T(1,128)} %owners_ref.1), custom_call_target="tpu_custom_call" | custom-call | flops 100000000 | bytes 400000 | tf_op jit(solution)/shard_map/pallas_call | solution.py:476
  143.8 1.3 copy.7
  145.2 1.5 %copy.9 = f32[8,16,128]{2,1,0:T(8,128)} copy(f32[8,16,128]{2,1,0:T(8,128)} %get-tuple-element.6) | data formatting | bytes 131072

commit v2 on v1

--- a/solution.py
+++ b/solution.py
@@ -157,11 +157,16 @@
     first_dev, last_dev = gz == 0, gz == n_z - 1
     zero_plane = jnp.zeros((1, nd, lanes), F32)
 
-    def loop(count, step, body):
+    def chunks(start, stop, body, step=16):
+        whole = (stop - start) // step
+
         def run(i, carry):
-            body(i * step)
+            body(start + i * step, step)
             return carry
-        lax.fori_loop(0, count // step, run, 0)
+
+        lax.fori_loop(0, whole, run, 0)
+        if (stop - start) % step:
+            body(start + whole * step, (stop - start) % step)
 
     def pads(ref):
         ref[0:1] = zero_plane
@@ -171,32 +176,32 @@
         pads(ref)
 
     def level(c, length, halo, own, scale, m, xr, yr, zr, dr, ir):
-        za = scale * ANISO
-        zr[length : length + 1] = zero_plane
-
-        def body(i):
-            k = i
-            here = c[pl.ds(k + 1, 1)]
-            below, above = c[pl.ds(k, 1)], c[pl.ds(k + 2, 1)]
-            cut_lo = (k == 0) | (first_dev & (k == halo)) | (last_dev & (k == halo + own))
-            cut_hi = (k == length - 1) | (first_dev & (k == halo - 1)) | (
-                last_dev & (k == halo + own - 1))
-            keep_lo = jnp.where(cut_lo, 0.0, 0.5 * za)
-            keep_hi = jnp.where(cut_hi, 0.0, 0.5 * za)
-            edge_z = jnp.where(cut_lo, za, 0.0) + jnp.where(cut_hi, za, 0.0)
-            wz = keep_lo * (below + here)
-            zr[pl.ds(k, 1)] = wz
+        half = 0.5 * scale * ANISO
+        c[0:1], c[length + 1 :] = c[1:2], c[length : length + 1]
+        lo, hi = halo, halo + own + 1
+        c[lo : lo + 1] = jnp.where(first_dev, c[lo + 1 : lo + 2], c[lo : lo + 1])
+        c[hi : hi + 1] = jnp.where(last_dev, c[hi - 1 : hi], c[hi : hi + 1])
+
+        def body(k, n):
+            here = c[pl.ds(k + 1, n)]
+            wz = half * (c[pl.ds(k, n)] + here)
+            zr[pl.ds(k, n)] = wz
             wx = (scale * m["xin"]) * (here + x_next(here, m))
             wy = (scale * m["yin"]) * (here + y_next(here, m))
             diag = wx + x_prev(wx, m) + wy + y_prev(wy, m) + (scale * m["edge"]) * here
-            diag = diag + wz + keep_hi * (above + here) + edge_z * here
-            dr[pl.ds(k, 1)] = diag
+            diag = diag + wz + half * (c[pl.ds(k + 2, n)] + here)
+            dr[pl.ds(k, n)] = diag
             if xr is not None:
-                xr[pl.ds(k, 1)] = wx
-                yr[pl.ds(k, 1)] = wy
-                ir[pl.ds(k, 1)] = OMEGA / diag
-
-        loop(length, 1, body)
+                xr[pl.ds(k, n)] = wx
+                yr[pl.ds(k, n)] = wy
+                ir[pl.ds(k, n)] = OMEGA / diag
+
+        chunks(0, length, body)
+        zr[0:1] = zero_plane
+        zr[length : length + 1] = zero_plane
+        lo, hi = halo, halo + own
+        zr[lo : lo + 1] = jnp.where(first_dev, 0.0, zr[lo : lo + 1])
+        zr[hi : hi + 1] = jnp.where(last_dev, 0.0, zr[hi : hi + 1])
 
     def pull(v, k, step, m, xr, yr, zr):
         here = v[pl.ds(k + 1, step)]
@@ -207,13 +212,12 @@
         total = total + (wy * y_next(here, m) + y_prev(wy * here, m))
         return here, total
 
-    def sweep(v, out, b, start, stop, m, xr, yr, zr, ir, step=4):
-        def body(i):
-            k = start + i
-            here, total = pull(v, k, step, m, xr, yr, zr)
-            out[pl.ds(k + 1, step)] = (1.0 - OMEGA) * here + ir[pl.ds(k, step)] * (
-                b[pl.ds(k, step)] + total)
-        loop(stop - start, step, body)
+    def sweep(v, out, b, start, stop, m, xr, yr, zr, ir):
+        def body(k, n):
+            here, total = pull(v, k, n, m, xr, yr, zr)
+            out[pl.ds(k + 1, n)] = (1.0 - OMEGA) * here + ir[pl.ds(k, n)] * (
+                b[pl.ds(k, n)] + total)
+        chunks(start, stop, body)
 
     fine = (m0, x0, y0, z0)
     mid = (m1, x1, y1, z1)
@@ -228,19 +232,17 @@
     def plane(row):
         return flat[pl.ds(row, nd, stride=gath.shape[1]), :][None]
 
-    def spread(i):
-        c0[pl.ds(1 + HALO + i, 1)] = plane(i)
-        b0[pl.ds(HALO + i, 1)] = plane(cz_len + i)
-
-    loop(cz_len, 1, spread)
-
-    def spread_halo(i):
-        c0[pl.ds(1 + i, 1)] = plane(base_lo + SEND - HALO + i)
-        b0[pl.ds(i, 1)] = plane(base_lo + 2 * SEND - HALO + i)
-        c0[pl.ds(1 + HALO + cz_len + i, 1)] = plane(base_hi + i)
-        b0[pl.ds(HALO + cz_len + i, 1)] = plane(base_hi + SEND + i)
-
-    loop(HALO, 1, spread_halo)
+    def spread(i, n):
+        for u in range(n):
+            c0[pl.ds(1 + HALO + i + u, 1)] = plane(i + u)
+            b0[pl.ds(HALO + i + u, 1)] = plane(cz_len + i + u)
+
+    chunks(0, cz_len, spread)
+    for i in range(HALO):
+        c0[1 + i : 2 + i] = plane(base_lo + SEND - HALO + i)
+        b0[i : 1 + i] = plane(base_lo + 2 * SEND - HALO + i)
+        c0[1 + HALO + cz_len + i : 2 + HALO + cz_len + i] = plane(base_hi + i)
+        b0[HALO + cz_len + i : 1 + HALO + cz_len + i] = plane(base_hi + SEND + i)
 
     states = []
     for k in range(1, nd):
@@ -255,45 +257,43 @@
         v = ref[pl.ds(k, 2 * step)].reshape(step, 2, nd, lanes)
         return v[:, 0] + v[:, 1]
 
-    def coarsen1(K):
-        c1[pl.ds(K + 1, 2)] = block_mean(pairs(c0, 1 + 2 * K, 2), m0)
-
-    loop(Z1, 2, coarsen1)
-
-    def coarsen2(K):
-        c2[pl.ds(K + 1, 2)] = block_mean(pairs(c1, 1 + H1 - 2 + 2 * K, 2), m1)
-
-    loop(Z2, 2, coarsen2)
+    def coarsen1(K, n):
+        c1[pl.ds(K + 1, n)] = block_mean(pairs(c0, 1 + 2 * K, n), m0)
+
+    chunks(0, Z1, coarsen1)
+
+    def coarsen2(K, n):
+        c2[pl.ds(K + 1, n)] = block_mean(pairs(c1, 1 + H1 - 2 + 2 * K, n), m1)
+
+    chunks(0, Z2, coarsen2)
     level(c0, Z0, HALO, cz_len, 1.0, m0, x0, y0, z0, d0, i0)
     level(c1, Z1, H1, L1, 0.25, m1, x1, y1, z1, d1, i1)
     level(c2, Z2, 1, L2, 0.0625, m2, None, None, z2, d2, None)
 
-    def first0(k):
-        va[pl.ds(k + 1, 4)] = i0[pl.ds(k, 4)] * b0[pl.ds(k, 4)]
-
-    loop(Z0, 4, first0)
-    sweep(va, vb, b0, 2, Z0 - 2, *fine, i0)
+    def first0(k, n):
+        va[pl.ds(k + 1, n)] = i0[pl.ds(k, n)] * b0[pl.ds(k, n)]
+
+    chunks(0, Z0, first0)
+    sweep(va, vb, b0, 1, Z0 - 1, *fine, i0)
     sweep(vb, va, b0, 2, Z0 - 2, *fine, i0)
 
-    def resid0_all():
-        def body(i):
-            K = 2 + i
-            k = 2 * K
-            here, total = pull(va, k, 4, *fine)
-            r = b0[pl.ds(k, 4)] + total - d0[pl.ds(k, 4)] * here
-            r = r.reshape(2, 2, nd, lanes)
-            b1[pl.ds(K, 2)] = block_mean(r[:, 0] + r[:, 1], m0)
-        loop(Z1 - 4, 2, body)
-
-    resid0_all()
-
-    def first1(i):
-        k = 2 + i
-        ma[pl.ds(k + 1, 2)] = i1[pl.ds(k, 2)] * b1[pl.ds(k, 2)]
-
-    loop(Z1 - 4, 2, first1)
+    def residual(v, b, d, k, n, m, *weights):
+        here, total = pull(v, k, 2 * n, m, *weights)
+        r = b[pl.ds(k, 2 * n)] + total - d[pl.ds(k, 2 * n)] * here
+        r = r.reshape(n, 2, nd, lanes)
+        return block_mean(r[:, 0] + r[:, 1], m)
+
+    def resid0(K, n):
+        b1[pl.ds(K, n)] = residual(va, b0, d0, 2 * K, n, *fine)
+
+    chunks(2, Z1 - 2, resid0, 8)
+
+    def first1(k, n):
+        ma[pl.ds(k + 1, n)] = i1[pl.ds(k, n)] * b1[pl.ds(k, n)]
+
+    chunks(2, Z1 - 2, first1)
     sweep(ma, mb, b1, 3, Z1 - 3, *mid, i1)
-    sweep(mb, ma, b1, 3, Z1 - 3, *mid, i1)
+    sweep(mb, ma, b1, 4, Z1 - 4, *mid, i1)
 
     mids = [
         copy(ma.at[pl.ds(1 + L1, H1)], mid_lo.at[0], mid_send.at[0], mid_recv.at[0], (gx, gy, up)),
@@ -302,18 +302,27 @@
         copy(b1.at[pl.ds(H1, H1)], mid_hi.at[1], mid_send.at[3], mid_recv.at[3], (gx, gy, down)),
     ]
 
-    def resid1(K):
-        k = H1 + 2 * K
-        here, total = pull(ma, k, 4, *mid)
-        r = b1[pl.ds(k, 4)] + total - d1[pl.ds(k, 4)] * here
-        r = r.reshape(2, 2, nd, lanes)
-        r2[pl.ds(K, 2)] = block_mean(r[:, 0] + r[:, 1], m1)
-
-    loop(L2, 2, resid1)
+    def resid1(K, n):
+        r2[pl.ds(K, n)] = residual(ma, b1, d1, H1 + 2 * K, n, *mid)
+
+    chunks(0, L2, resid1, 8)
 
     inv = 1.0 / d2[1]
     y_now, p_now = r2[0], jnp.ones((nd, lanes), F32)
     im2[0], spike[0, 0], spike[1, 0] = inv, y_now, p_now
+
+    def chain(start, stop, step, carry, turn=4):
+        whole = (stop - start) // turn
+
+        def run(i, carry):
+            for u in range(turn):
+                carry = step(start + i * turn + u, carry)
+            return carry
+
+        carry = lax.fori_loop(0, whole, run, carry)
+        for k in range(start + whole * turn, stop):
+            carry = step(k, carry)
+        return carry
 
     def forward(k, carry):
         inv, y_now, p_now = carry
@@ -325,7 +334,7 @@
         im2[k], spike[0, k], spike[1, k] = inv, y_now, p_now
         return inv, y_now, p_now
 
-    inv, y_now, p_now = lax.fori_loop(1, L2, forward, (inv, y_now, p_now))
+    inv, y_now, p_now = chain(1, L2, forward, (inv, y_now, p_now))
     last = (y_now * inv, p_now * inv, inv)
     for i in range(3):
         spike[i, L2 - 1] = last[i]
@@ -340,7 +349,7 @@
         spike[0, k], spike[1, k], spike[2, k] = g, p, q
         return g, p, q
 
-    head = lax.fori_loop(0, L2 - 1, backward, last)
+    head = chain(0, L2 - 1, backward, last)
     for i in range(3):
         iface[gz, i] = head[i]
         iface[gz, 3 + i] = last[i]
@@ -360,10 +369,11 @@
     def splane(row):
         return sflat[pl.ds(row, nd, stride=sgath.shape[1]), :][None]
 
-    def spread_state(i):
-        s0[pl.ds(1 + i, 1)] = splane(i)
-
-    loop(cz_len, 1, spread_state)
+    def spread_state(i, n):
+        for u in range(n):
+            s0[pl.ds(1 + i + u, 1)] = splane(i + u)
+
+    chunks(0, cz_len, spread_state)
     s0[0:1] = jnp.where(first_dev, 0.0, splane(cz_len + 7))
     s0[cz_len + 1 :] = jnp.where(last_dev, 0.0, splane(cz_len + 8))
 
@@ -398,12 +408,12 @@
         return jnp.broadcast_to(v[:, None], (v.shape[0], 2, nd, lanes)).reshape(
             2 * v.shape[0], nd, lanes)
 
-    def correct(K):
-        x = spike[0, pl.ds(K, 2)] + spike[1, pl.ds(K, 2)] * L + spike[2, pl.ds(K, 2)] * R
+    def correct(K, n):
+        x = spike[0, pl.ds(K, n)] + spike[1, pl.ds(K, n)] * L + spike[2, pl.ds(K, n)] * R
         k = 1 + H1 + 2 * K
-        ma[pl.ds(k, 4)] = ma[pl.ds(k, 4)] + twice(x)
-
-    loop(L2, 2, correct)
+        ma[pl.ds(k, 2 * n)] = ma[pl.ds(k, 2 * n)] + twice(x)
+
+    chunks(0, L2, correct, 8)
     xl = spk_lo[0] + spk_lo[1] * sides[down, 0] + spk_lo[2] * sides[down, 1]
     ma[1 : 1 + H1] = mid_lo[0] + twice(xl)[6 - H1 :]
     b1[0:H1] = mid_lo[1]
@@ -412,32 +422,32 @@
     b1[H1 + L1 :] = mid_hi[1]
 
     sweep(ma, mb, b1, 1, Z1 - 1, *mid, i1)
-    sweep(mb, ma, b1, 1, Z1 - 1, *mid, i1)
+    sweep(mb, ma, b1, 2, Z1 - 2, *mid, i1)
     sweep(ma, mb, b1, 3, Z1 - 3, *mid, i1)
 
-    def raise0(i):
-        K = 3 + i
+    def raise0(K, n):
         k = 1 + 2 * K
-        va[pl.ds(k, 4)] = va[pl.ds(k, 4)] + twice(mb[pl.ds(K + 1, 2)])
-
-    loop(Z1 - 6, 2, raise0)
-    sweep(va, vb, b0, HALO - 4, HALO + cz_len + 4, *fine, i0)
+        va[pl.ds(k, 2 * n)] = va[pl.ds(k, 2 * n)] + twice(mb[pl.ds(K + 1, n)])
+
+    chunks(3, Z1 - 3, raise0, 8)
+    sweep(va, vb, b0, HALO - 3, HALO + cz_len + 3, *fine, i0)
     sweep(vb, va, b0, HALO - 2, HALO + cz_len + 2, *fine, i0)
-    sweep(va, vb, b0, HALO - 2, HALO + cz_len + 2, *fine, i0)
-
-    def terms(i, acc):
-        a, s = vb[pl.ds(HALO + 1 + i, 1)], s0[pl.ds(1 + i, 1)]
+    sweep(va, vb, b0, HALO - 1, HALO + cz_len + 1, *fine, i0)
+
+    lo, hi = HALO, HALO + cz_len + 1
+    vb[lo : lo + 1] = jnp.where(first_dev, -vb[lo + 1 : lo + 2], vb[lo : lo + 1])
+    vb[hi : hi + 1] = jnp.where(last_dev, -vb[hi - 1 : hi], vb[hi : hi + 1])
+
+    def terms(i, n):
+        a, s = vb[pl.ds(HALO + 1 + i, n)], s0[pl.ds(1 + i, n)]
         tx = m0["xin"] * ((a - x_next(a, m0)) * (s - x_next(s, m0)))
         ty = m0["yin"] * ((a - y_next(a, m0)) * (s - y_next(s, m0)))
         t = tx + x_prev(tx, m0) + ty + y_prev(ty, m0) + m0["edge"] * (a * s)
-        lo = first_dev & (i == 0)
-        hi = last_dev & (i == cz_len - 1)
-        below, above = vb[pl.ds(HALO + i, 1)], vb[pl.ds(HALO + 2 + i, 1)]
-        t = t + jnp.where(lo, a * s, 0.5 * ((a - below) * (s - s0[pl.ds(i, 1)])))
-        t = t + jnp.where(hi, a * s, 0.5 * ((a - above) * (s - s0[pl.ds(2 + i, 1)])))
-        return acc + (c0[pl.ds(HALO + 1 + i, 1)] * t)[0]
-
-    acc = lax.fori_loop(0, cz_len, terms, zero)
+        z = (a - vb[pl.ds(HALO + i, n)]) * (s - s0[pl.ds(i, n)])
+        z = z + (a - vb[pl.ds(HALO + 2 + i, n)]) * (s - s0[pl.ds(2 + i, n)])
+        return jnp.sum(c0[pl.ds(HALO + 1 + i, n)] * (t + 0.5 * z), axis=0)
+
+    acc = lax.fori_loop(0, cz_len // 16, lambda i, acc: acc + terms(16 * i, 16), zero)
     part[gz] = acc
     parts = []
     for j in range(1, n_z):

time: 147 us -> 64.1 us (0.44)
  Pallas kernels: 143 us -> 60.4 us
    pallas_call x1, Pallas kernels: 143 us -> 60.4 us  [per_device(): pl.pallas_call(functools.partial(kernel, n_x, n_y, n_z, cx, cy, cz, cz *...]
where the time goes in v2:
time: 64.1 us; the launch traced here: 63.8 us
  Pallas kernels  60.4 us (94%)
  local copies, waits for them, and re-layouts  2.8 us (4%)
    pallas_call x1, Pallas kernels, per_device(): pl.pallas_call(functools.partial(kernel, n_x, n_y, n_z, cx, cy, cz, cz *...  60.4 us
    unnamed x1, local copies, waits for them, and re-layouts  1.47 us
    pallas_call x1, local copies, waits for them, and re-layouts, per_device(): pl.pallas_call(functools.partial(kernel, n_x, n_y, n_z, cx, cy, cz, cz *...  1.33 us

profile of v2, /device:TPU:0, one launch (start us, length us, event | category | flops | bytes accessed | tf_op | source)
XLA Modules:
  0.0 63.8 jit_solution(15816708402388335833)
XLA Ops:
  0.6 60.4 %shard_map.68 = (f32[8,16,128]{2,1,0:T(8,128)}, f32[8,4]{1,0:T(8,128)}) custom-call(f32[8,16,128]{2,1,0:T(8,128)} %source_ref.1, f32[8,16,128]{2,1,0:T(8,128)} %state_ref.1, f32[8,16,128]{2,1,0:T(8,128)} %logc_ref.1, f32[8,16]{1,0:T(8,128)} %lat_ref.1, s32[1,1,4]{2,1,0:T(1,128)} %owners_ref.1), custom_call_target="tpu_custom_call" | custom-call | flops 100000000 | bytes 400000 | tf_op jit(solution)/shard_map/pallas_call | solution.py:486
  61.0 1.3 %copy.7 = f32[8,4]{0,1:T(4,128)} copy(f32[8,4]{1,0:T(8,128)} %get-tuple-element.3) | data formatting | bytes 256 | tf_op jit(solution)/shard_map/pallas_call | solution.py:486
  62.4 1.5 %copy.9 = f32[8,16,128]{2,1,0:T(8,128)} copy(f32[8,16,128]{2,1,0:T(8,128)} %get-tuple-element.6) | data formatting | bytes 131072

commit v3 on v2

--- a/solution.py
+++ b/solution.py
@@ -21,11 +21,11 @@
     source_ref, state_ref, logc_ref, lat_ref, owners_ref,
     adj_ref, grad_ref,
     gath, sgath, stage_lo, stage_hi, sstage_lo, sstage_hi,
-    c0, x0, y0, z0, d0, i0, b0, va, vb,
-    c1, x1, y1, z1, d1, i1, b1, ma, mb,
+    c0, x0, w0, y0, z0, d0, i0, b0, va, vb,
+    c1, x1, w1, y1, z1, d1, i1, b1, ma, mb,
     c2, z2, d2, r2, im2, spike,
     s0, iface, sides, mid_lo, mid_hi, spk_lo, spk_hi, part,
-    main_send, main_recv, lo_send, lo_recv, hi_send, hi_recv,
+    main_send, main_recv, src_send, src_recv, lo_send, lo_recv, hi_send, hi_recv,
     st_send, st_recv, stz_send, stz_recv,
     mid_send, mid_recv, if_send, if_recv, pt_send, pt_recv,
 ):
@@ -51,32 +51,38 @@
 
     lane = lax.broadcasted_iota(jnp.int32, (nd, lanes), 1)
     sub = lax.broadcasted_iota(jnp.int32, (nd, lanes), 0)
-    xs, ys = lane // cy_len, lane % cy_len
-    dx, dy = sub // n_y, sub % n_y
+    y_all = n_y * cy_len
+    x_row = lanes // y_all
+    xm, ys = lane // y_all, lane % y_all
+    xs = sub * x_row + xm
+    slot = ys // cy_len - sub % n_y
     lane8 = lax.broadcasted_iota(jnp.int32, (cx_len, lanes), 1)
     row8 = lax.broadcasted_iota(jnp.int32, (cx_len, lanes), 0)
     lat = jnp.zeros((cx_len, lanes), F32)
     for y in range(cy_len):
         lat = jnp.where(lane8 % cy_len == y, lat_ref[:, y : y + 1], lat)
-    lat = jnp.sum(jnp.where(lane8 // cy_len == row8, lat, 0.0), axis=0, keepdims=True)
+    lane_x = lane8 // cy_len % n_y * x_row + lane8 // y_all
+    lat = jnp.sum(jnp.where(lane_x == row8, lat, 0.0), axis=0, keepdims=True)
 
     def rows_of(ref):
-        return ref[...].reshape(lanes, cz_len).T
+        v = ref[...].reshape(n_y, x_row, cy_len, cz_len)
+        v = jnp.stack([v[:, i] for i in range(x_row)])
+        return v.reshape(lanes, cz_len).T
 
     coef = jnp.exp(rows_of(logc_ref) + lat)
     src = rows_of(source_ref)
     state = rows_of(state_ref)
     gath[me, 0:cz_len, :] = coef
-    gath[me, cz_len : 2 * cz_len, :] = src
+    gath[me, cz_len + 16 : 2 * cz_len + 16, :] = src
     line = owners_ref[0]
     for j in range(16):
         if 0 < j < n_z:
             same = jnp.broadcast_to(line[:, j : j + 1], (1, lanes)) == jnp.broadcast_to(
                 line[:, j - 1 : j], (1, lanes)
             )
-            gath[me, 2 * cz_len + j : 2 * cz_len + j + 1, :] = jnp.where(same, 1.0, 0.0)
+            gath[me, cz_len + j : cz_len + j + 1, :] = jnp.where(same, 1.0, 0.0)
         else:
-            gath[me, 2 * cz_len + j : 2 * cz_len + j + 1, :] = jnp.zeros((1, lanes), F32)
+            gath[me, cz_len + j : cz_len + j + 1, :] = jnp.zeros((1, lanes), F32)
     stage_lo[0:SEND, :] = coef[cz_len - SEND :]
     stage_lo[SEND : 2 * SEND, :] = src[cz_len - SEND :]
     stage_hi[0:SEND, :] = coef[:SEND]
@@ -100,58 +106,73 @@
 
     main, los, his = [], [], []
     for k in range(1, nd):
-        body = gath.at[me, pl.ds(0, base_lo)]
+        body = gath.at[me, pl.ds(0, cz_len + 16)]
         main.append(copy(body, body, main_send.at[k], main_recv.at[k], place(k, gz)))
     for k in range(nd):
         los.append(copy(stage_lo, gath.at[me, pl.ds(base_lo, 2 * SEND)],
                         lo_send.at[k], lo_recv.at[k], place(k, up)))
         his.append(copy(stage_hi, gath.at[me, pl.ds(base_hi, 2 * SEND)],
                         hi_send.at[k], hi_recv.at[k], place(k, down)))
+    sources = []
+    for k in range(1, nd):
+        body = gath.at[me, pl.ds(cz_len + 16, cz_len)]
+        sources.append(copy(body, body, src_send.at[k], src_recv.at[k], place(k, gz)))
 
     def roll(v, shift, axis):
         return pltpu.roll(v, shift % v.shape[axis], axis)
 
+    nx_all = n_x * cx_len
+
     def masks(s):
+        ends_x = jnp.where(xs < s, 1.0, 0.0) + jnp.where(xs >= nx_all - s, 1.0, 0.0)
+        ends_y = jnp.where(ys < s, 1.0, 0.0) + jnp.where(ys >= y_all - s, 1.0, 0.0)
         return dict(
-            s=s,
-            xhi=(xs >= cx_len - s)[None], xlo=(xs < s)[None],
-            yhi=(ys >= cy_len - s)[None], ylo=(ys < s)[None],
-            xin=jnp.where((xs >= cx_len - s) & (dx == n_x - 1), 0.0, 0.5)[None],
-            yin=jnp.where((ys >= cy_len - s) & (dy == n_y - 1), 0.0, 0.5)[None],
-            edge=(
-                jnp.where((xs >= cx_len - s) & (dx == n_x - 1), 1.0, 0.0)
-                + jnp.where((xs < s) & (dx == 0), 1.0, 0.0)
-                + jnp.where((ys >= cy_len - s) & (dy == n_y - 1), 1.0, 0.0)
-                + jnp.where((ys < s) & (dy == 0), 1.0, 0.0)
-            )[None],
+            s=s, xhi=(xm >= x_row - s)[None], xlo=(xm < s)[None],
+            xin=jnp.where(xs >= nx_all - s, 0.0, 0.5)[None],
+            yin=jnp.where(ys >= y_all - s, 0.0, 0.5)[None],
+            edge=(ends_x + ends_y)[None],
             xbit=(xs // s % 2 == 0)[None], ybit=(ys // s % 2 == 0)[None],
         )
 
     def pick(mask, a, b):
         return jnp.where(jnp.broadcast_to(mask, a.shape), a, b)
 
-    def x_next(v, m):
-        r = roll(v, -m["s"] * cy_len, 2)
-        return pick(m["xhi"], roll(r, -n_y, 1), r)
-
-    def x_prev(v, m):
-        r = roll(v, m["s"] * cy_len, 2)
-        return pick(m["xlo"], roll(r, n_y, 1), r)
+    def x_next(v, m, row=None):
+        s = m["s"]
+        if s >= x_row:
+            return roll(v, -(s // x_row), 1)
+        row = roll(v, -1, 1) if row is None else row
+        return roll(pick(m["xlo"], row, v), -s * y_all, 2)
+
+    def x_prev(v, m, row=None):
+        s = m["s"]
+        if s >= x_row:
+            return roll(v, s // x_row, 1)
+        row = roll(v, 1, 1) if row is None else row
+        return roll(pick(m["xhi"], row, v), s * y_all, 2)
 
     def y_next(v, m):
-        r = roll(v, -m["s"], 2)
-        return pick(m["yhi"], roll(roll(v, -1, 1), cy_len - m["s"], 2), r)
+        return roll(v, -m["s"], 2)
 
     def y_prev(v, m):
-        r = roll(v, m["s"], 2)
-        return pick(m["ylo"], roll(roll(v, 1, 1), m["s"] - cy_len, 2), r)
+        return roll(v, m["s"], 2)
 
     def block_mean(pair, m):
         s = m["s"]
         v = pair + pick(m["ybit"], roll(pair, -s, 2), roll(pair, s, 2))
-        w = s * cy_len
-        v = v + pick(m["xbit"], roll(v, -w, 2), roll(v, w, 2))
-        return 0.125 * v
+        if s >= x_row:
+            near, far = roll(v, -(s // x_row), 1), roll(v, s // x_row, 1)
+        else:
+            near, far = roll(v, -s * y_all, 2), roll(v, s * y_all, 2)
+        return 0.125 * (v + pick(m["xbit"], near, far))
+
+    def to_plane(v):
+        out = v
+        for shift in range(1 - n_y, n_y):
+            if shift:
+                moved = roll(roll(v, -shift, 1), shift * cy_len, 2)
+                out = pick((slot == shift)[None], moved, out)
+        return out
 
     m0, m1, m2 = masks(1), masks(2), masks(4)
     first_dev, last_dev = gz == 0, gz == n_z - 1
@@ -175,7 +196,7 @@
     for ref in (c0, va, vb, c1, ma, mb, c2):
         pads(ref)
 
-    def level(c, length, halo, own, scale, m, xr, yr, zr, dr, ir):
+    def level(c, length, halo, own, scale, m, xr, wr, yr, zr, dr, ir):
         half = 0.5 * scale * ANISO
         c[0:1], c[length + 1 :] = c[1:2], c[length : length + 1]
         lo, hi = halo, halo + own + 1
@@ -188,11 +209,13 @@
             zr[pl.ds(k, n)] = wz
             wx = (scale * m["xin"]) * (here + x_next(here, m))
             wy = (scale * m["yin"]) * (here + y_next(here, m))
-            diag = wx + x_prev(wx, m) + wy + y_prev(wy, m) + (scale * m["edge"]) * here
+            wp = x_prev(wx, m)
+            diag = wx + wp + wy + y_prev(wy, m) + (scale * m["edge"]) * here
             diag = diag + wz + half * (c[pl.ds(k + 2, n)] + here)
             dr[pl.ds(k, n)] = diag
             if xr is not None:
                 xr[pl.ds(k, n)] = wx
+                wr[pl.ds(k, n)] = wp
                 yr[pl.ds(k, n)] = wy
                 ir[pl.ds(k, n)] = OMEGA / diag
 
@@ -203,24 +226,31 @@
         zr[lo : lo + 1] = jnp.where(first_dev, 0.0, zr[lo : lo + 1])
         zr[hi : hi + 1] = jnp.where(last_dev, 0.0, zr[hi : hi + 1])
 
-    def pull(v, k, step, m, xr, yr, zr):
-        here = v[pl.ds(k + 1, step)]
-        wx, wy = xr[pl.ds(k, step)], yr[pl.ds(k, step)]
-        total = zr[pl.ds(k, step)] * v[pl.ds(k, step)]
-        total = total + zr[pl.ds(k + 1, step)] * v[pl.ds(k + 2, step)]
-        total = total + (wx * x_next(here, m) + x_prev(wx * here, m))
+    def pull(v, k, n, m, xr, wr, yr, zr):
+        near, wz = v[pl.ds(k, n + 2)], zr[pl.ds(k, n + 1)]
+        here = near[1 : n + 1]
+        if m["s"] < x_row:
+            rows = v.reshape(v.shape[0] * nd, lanes)
+            later = rows[pl.ds((k + 1) * nd + 1, n * nd), :].reshape(n, nd, lanes)
+            prior = rows[pl.ds((k + 1) * nd - 1, n * nd), :].reshape(n, nd, lanes)
+        else:
+            later = prior = None
+        wy = yr[pl.ds(k, n)]
+        total = wz[:n] * near[:n] + wz[1:] * near[2:]
         total = total + (wy * y_next(here, m) + y_prev(wy * here, m))
+        total = total + xr[pl.ds(k, n)] * x_next(here, m, later)
+        total = total + wr[pl.ds(k, n)] * x_prev(here, m, prior)
         return here, total
 
-    def sweep(v, out, b, start, stop, m, xr, yr, zr, ir):
+    def sweep(v, out, b, start, stop, m, xr, wr, yr, zr, ir):
         def body(k, n):
-            here, total = pull(v, k, n, m, xr, yr, zr)
+            here, total = pull(v, k, n, m, xr, wr, yr, zr)
             out[pl.ds(k + 1, n)] = (1.0 - OMEGA) * here + ir[pl.ds(k, n)] * (
                 b[pl.ds(k, n)] + total)
         chunks(start, stop, body)
 
-    fine = (m0, x0, y0, z0)
-    mid = (m1, x1, y1, z1)
+    fine = (m0, x0, w0, y0, z0)
+    mid = (m1, x1, w1, y1, z1)
 
     for c in main:
         c.wait()
@@ -229,20 +259,46 @@
     flat = gath.reshape(nd * gath.shape[1], lanes)
     sflat = sgath.reshape(nd * sgath.shape[1], lanes)
 
-    def plane(row):
-        return flat[pl.ds(row, nd, stride=gath.shape[1]), :][None]
+    def planes(rows, height, start, n):
+        return to_plane(jnp.stack(
+            [rows[pl.ds(start + u, nd, stride=height), :] for u in range(n)]))
+
+    def gplanes(start, n):
+        return planes(flat, gath.shape[1], start, n)
 
     def spread(i, n):
-        for u in range(n):
-            c0[pl.ds(1 + HALO + i + u, 1)] = plane(i + u)
-            b0[pl.ds(HALO + i + u, 1)] = plane(cz_len + i + u)
+        c0[pl.ds(1 + HALO + i, n)] = gplanes(i, n)
 
     chunks(0, cz_len, spread)
-    for i in range(HALO):
-        c0[1 + i : 2 + i] = plane(base_lo + SEND - HALO + i)
-        b0[i : 1 + i] = plane(base_lo + 2 * SEND - HALO + i)
-        c0[1 + HALO + cz_len + i : 2 + HALO + cz_len + i] = plane(base_hi + i)
-        b0[HALO + cz_len + i : 1 + HALO + cz_len + i] = plane(base_hi + SEND + i)
+    c0[1 : 1 + HALO] = gplanes(base_lo + SEND - HALO, HALO)
+    b0[0:HALO] = gplanes(base_lo + 2 * SEND - HALO, HALO)
+    c0[1 + HALO + cz_len : 1 + 2 * HALO + cz_len] = gplanes(base_hi, HALO)
+    b0[HALO + cz_len :] = gplanes(base_hi + SEND, HALO)
+
+    def pairs(ref, k, step):
+        v = ref[pl.ds(k, 2 * step)].reshape(step, 2, nd, lanes)
+        return v[:, 0] + v[:, 1]
+
+    def coarsen1(K, n):
+        c1[pl.ds(K + 1, n)] = block_mean(pairs(c0, 1 + 2 * K, n), m0)
+
+    chunks(0, Z1, coarsen1)
+
+    def coarsen2(K, n):
+        c2[pl.ds(K + 1, n)] = block_mean(pairs(c1, 1 + H1 - 2 + 2 * K, n), m1)
+
+    chunks(0, Z2, coarsen2)
+    level(c0, Z0, HALO, cz_len, 1.0, m0, x0, w0, y0, z0, d0, i0)
+    level(c1, Z1, H1, L1, 0.25, m1, x1, w1, y1, z1, d1, i1)
+    level(c2, Z2, 1, L2, 0.0625, m2, None, None, None, z2, d2, None)
+
+    for c in sources:
+        c.wait()
+
+    def spread_source(i, n):
+        b0[pl.ds(HALO + i, n)] = gplanes(cz_len + 16 + i, n)
+
+    chunks(0, cz_len, spread_source)
 
     states = []
     for k in range(1, nd):
@@ -253,22 +309,6 @@
     states.append(copy(sstage_hi, sgath.at[me, pl.ds(cz_len + 8, 8)],
                        stz_send.at[1], stz_recv.at[1], (gx, gy, down)))
 
-    def pairs(ref, k, step):
-        v = ref[pl.ds(k, 2 * step)].reshape(step, 2, nd, lanes)
-        return v[:, 0] + v[:, 1]
-
-    def coarsen1(K, n):
-        c1[pl.ds(K + 1, n)] = block_mean(pairs(c0, 1 + 2 * K, n), m0)
-
-    chunks(0, Z1, coarsen1)
-
-    def coarsen2(K, n):
-        c2[pl.ds(K + 1, n)] = block_mean(pairs(c1, 1 + H1 - 2 + 2 * K, n), m1)
-
-    chunks(0, Z2, coarsen2)
-    level(c0, Z0, HALO, cz_len, 1.0, m0, x0, y0, z0, d0, i0)
-    level(c1, Z1, H1, L1, 0.25, m1, x1, y1, z1, d1, i1)
-    level(c2, Z2, 1, L2, 0.0625, m2, None, None, z2, d2, None)
 
     def first0(k, n):
         va[pl.ds(k + 1, n)] = i0[pl.ds(k, n)] * b0[pl.ds(k, n)]
@@ -353,7 +393,7 @@
     for i in range(3):
         iface[gz, i] = head[i]
         iface[gz, 3 + i] = last[i]
-    iface[gz, 6] = z2[1] * flat[pl.ds(2 * cz_len + gz, nd, stride=gath.shape[1]), :]
+    iface[gz, 6] = z2[1] * gplanes(cz_len + gz, 1)[0]
     ifs = []
     for j in range(1, n_z):
         ifs.append(copy(iface.at[gz], iface.at[gz], if_send.at[j], if_recv.at[j],
@@ -366,16 +406,15 @@
     for c in states:
         c.wait()
 
-    def splane(row):
-        return sflat[pl.ds(row, nd, stride=sgath.shape[1]), :][None]
+    def splanes(start, n):
+        return planes(sflat, sgath.shape[1], start, n)
 
     def spread_state(i, n):
-        for u in range(n):
-            s0[pl.ds(1 + i + u, 1)] = splane(i + u)
+        s0[pl.ds(1 + i, n)] = splanes(i, n)
 
     chunks(0, cz_len, spread_state)
-    s0[0:1] = jnp.where(first_dev, 0.0, splane(cz_len + 7))
-    s0[cz_len + 1 :] = jnp.where(last_dev, 0.0, splane(cz_len + 8))
+    s0[0:1] = jnp.where(first_dev, 0.0, splanes(cz_len + 7, 1))
+    s0[cz_len + 1 :] = jnp.where(last_dev, 0.0, splanes(cz_len + 8, 1))
 
     for c in mids + ifs:
         c.wait()
@@ -455,20 +494,31 @@
                           (gx, gy, lax.rem(gz + j, n_z))))
 
     vflat = vb.reshape(vb.shape[0] * nd, lanes)
-    own = vflat[pl.ds((HALO + 1) * nd + me, cz_len, stride=nd), :]
-    adj_ref[...] = own.T.reshape(cx_len, cy_len, cz_len)
+    own = jnp.zeros((cz_len, lanes), F32)
+    to_slot = lax.broadcasted_iota(jnp.int32, (cz_len, lanes), 1) // cy_len % n_y
+    for a in range(n_y):
+        row = vflat[pl.ds((HALO + 1) * nd + gx * n_y + a, cz_len, stride=nd), :]
+        moved = pltpu.roll(row, lax.rem((a - gy) * cy_len + lanes, lanes), 1)
+        own = jnp.where(to_slot == a, moved, own)
+    field = own.T.reshape(x_row, n_y, cy_len, cz_len)
+    for a in range(n_y):
+        for i in range(x_row):
+            adj_ref[a * x_row + i] = field[i, a]
 
     for c in parts:
         c.wait()
     total = part[0]
     for j in range(1, n_z):
         total = total + part[j]
-    row = jnp.sum(jnp.where(sub == me, total, 0.0), axis=0, keepdims=True)
-    row = jnp.broadcast_to(row, (cx_len, lanes)) * (-1.0 / math.sqrt(n_total))
+    rows = jnp.zeros((cx_len, lanes), F32)
+    for a in range(n_y):
+        row = jnp.sum(jnp.where(sub == gx * n_y + a, total, 0.0), axis=0, keepdims=True)
+        rows = jnp.where(row8 // x_row == a, jnp.broadcast_to(row, rows.shape), rows)
+    rows = rows * (-1.0 / math.sqrt(n_total))
     width = cy_len // n_z
     for j in range(width):
-        here = lane8 == row8 * cy_len + gz * width + j
-        grad_ref[:, j : j + 1] = jnp.sum(jnp.where(here, row, 0.0), axis=1, keepdims=True)
+        here = lane8 == row8 % x_row * y_all + gy * cy_len + gz * width + j
+        grad_ref[:, j : j + 1] = jnp.sum(jnp.where(here, rows, 0.0), axis=1, keepdims=True)
 
 
 def solution(mesh):
@@ -494,16 +544,16 @@
             scratch_shapes=[
                 V(nd, 2 * cz + 16 + 4 * SEND, lanes), V(nd, cz + 16, lanes),
                 V(2 * SEND, lanes), V(2 * SEND, lanes), V(8, lanes), V(8, lanes),
-                pln(Z0 + 2), pln(Z0), pln(Z0), pln(Z0 + 1), pln(Z0), pln(Z0), pln(Z0),
+                pln(Z0 + 2), pln(Z0), pln(Z0), pln(Z0), pln(Z0 + 1), pln(Z0), pln(Z0), pln(Z0),
                 pln(Z0 + 2), pln(Z0 + 2),
-                pln(Z1 + 2), pln(Z1), pln(Z1), pln(Z1 + 1), pln(Z1), pln(Z1), pln(Z1),
+                pln(Z1 + 2), pln(Z1), pln(Z1), pln(Z1), pln(Z1 + 1), pln(Z1), pln(Z1), pln(Z1),
                 pln(Z1 + 2), pln(Z1 + 2),
                 pln(Z2 + 2), pln(Z2 + 1), pln(Z2), pln(cz // 4), pln(cz // 4),
                 V(3, cz // 4, nd, lanes),
                 pln(cz + 2), V(n_z, 7, nd, lanes), V(n_z, 2, nd, lanes),
                 V(2, H1, nd, lanes), V(2, H1, nd, lanes),
                 V(3, 3, nd, lanes), V(3, 3, nd, lanes), V(n_z, nd, lanes),
-                D(nd), D(nd), D(nd), D(nd), D(nd), D(nd),
+                D(nd), D(nd), D(nd), D(nd), D(nd), D(nd), D(nd), D(nd),
                 D(nd), D(nd), D(2), D(2),
                 D(4), D(4), D(n_z + 2), D(n_z + 2), D(n_z), D(n_z),
             ],

time: 64.1 us -> 57.9 us (0.903)
  Pallas kernels: 60.4 us -> 54.2 us
    pallas_call x1, Pallas kernels: 60.4 us -> 54.2 us  [per_device(): pl.pallas_call(functools.partial(kernel, n_x, n_y, n_z, cx, cy, cz, cz *...]
where the time goes in v3:
time: 57.9 us; the launch traced here: 57.6 us
  Pallas kernels  54.2 us (94%)
  local copies, waits for them, and re-layouts  2.8 us (5%)
  between operations  0.64 us (1%)
    pallas_call x1, Pallas kernels, per_device(): pl.pallas_call(functools.partial(kernel, n_x, n_y, n_z, cx, cy, cz, cz *...  54.2 us
    unnamed x1, local copies, waits for them, and re-layouts  1.47 us
    pallas_call x1, local copies, waits for them, and re-layouts, per_device(): pl.pallas_call(functools.partial(kernel, n_x, n_y, n_z, cx, cy, cz, cz *...  1.33 us

profile of v3, /device:TPU:0, one launch (start us, length us, event | category | flops | bytes accessed | tf_op | source)
XLA Modules:
  0.0 57.6 jit_solution(10982921231028141124)
XLA Ops:
  0.6 54.2 %shard_map.68 = (f32[8,16,128]{2,1,0:T(8,128)}, f32[8,4]{1,0:T(8,128)}) custom-call(f32[8,16,128]{2,1,0:T(8,128)} %source_ref.1, f32[8,16,128]{2,1,0:T(8,128)} %state_ref.1, f32[8,16,128]{2,1,0:T(8,128)} %logc_ref.1, f32[8,16]{1,0:T(8,128)} %lat_ref.1, s32[1,1,4]{2,1,0:T(1,128)} %owners_ref.1), custom_call_target="tpu_custom_call" | custom-call | flops 100000000 | bytes 400000 | tf_op jit(solution)/shard_map/pallas_call | solution.py:536
  54.8 1.3 %copy.7 = f32[8,4]{0,1:T(4,128)} copy(f32[8,4]{1,0:T(8,128)} %get-tuple-element.3) | data formatting | bytes 256 | tf_op jit(solution)/shard_map/pallas_call | solution.py:536
  56.2 1.5 %copy.9 = f32[8,16,128]{2,1,0:T(8,128)} copy(f32[8,16,128]{2,1,0:T(8,128)} %get-tuple-element.6) | data formatting | bytes 131072

commit v4 on v3

v4 whole, which is shorter than its diff:
```python
import functools
import math

import jax
import jax.numpy as jnp
from jax import lax
from jax.experimental import pallas as pl
from jax.experimental.pallas import tpu as pltpu
from jax.sharding import PartitionSpec as P

ANISO = 200.0
OMEGA = 0.8
HALO = 10
SEND = 16
MESH = pl.DeviceIdType.MESH
F32 = jnp.float32


def kernel(
    n_x, n_y, n_z, cx_len, cy_len, cz_len, n_total,
    source_ref, state_ref, logc_ref, lat_ref, owners_ref,
    adj_ref, grad_ref,
    ext, stage, gath,
    c0, x0, w0, y0, z0, d0, i0, b0, va, vb,
    c1, x1, w1, y1, z1, d1, i1, b1, ma, mb,
    c2, z2, d2, low, rlow, fac, spike, corr,
    s0, iface, sides, mid_lo, mid_hi, spk_lo, spk_hi, outs, fin, part,
    z_send, z_recv, main_send, main_recv, st_send, st_recv,
    low_send, low_recv, r_send, r_recv,
    mid_send, mid_recv, if_send, if_recv, fin_send, fin_recv, pt_send, pt_recv,
):
    nd = n_x * n_y
    lanes = cx_len * cy_len
    gx, gy, gz = lax.axis_index("gx"), lax.axis_index("gy"), lax.axis_index("gz")
    me = gx * n_y + gy
    up, down = lax.rem(gz + 1, n_z), lax.rem(gz + n_z - 1, n_z)
    parts_n = min(nd, 8)
    own_n = cz_len // parts_n
    mine = lax.rem(me, parts_n)
    group = me - mine
    Z0, Z1, Z2 = own_n + 2 * HALO, own_n // 2 + HALO, own_n // 4 + 2
    H1 = HALO // 2
    L1, L2, NL = own_n // 2, own_n // 4, cz_len // 4
    WIN = own_n + 2 * SEND

    def place(k, z):
        peer = lax.rem(me + k, nd)
        return (lax.div(peer, n_y), lax.rem(peer, n_y), z)

    def member(k):
        peer = group + lax.rem(mine + k, parts_n)
        return peer, (lax.div(peer, n_y), lax.rem(peer, n_y), gz)

    def along(step):
        t = lax.rem(gz * parts_n + mine + step + n_z * parts_n, n_z * parts_n)
        peer = group + lax.rem(t, parts_n)
        return (lax.div(peer, n_y), lax.rem(peer, n_y), lax.div(t, parts_n))

    barrier = pltpu.get_barrier_semaphore()
    greeted = [place(k, gz) for k in range(1, nd)]
    greeted += [(gx, gy, lax.rem(gz + j, n_z)) for j in range(1, n_z)]
    greeted += [along(1), along(-1)]
    for device in greeted:
        pl.semaphore_signal(barrier, inc=1, device_id=device, device_id_type=MESH)

    lane = lax.broadcasted_iota(jnp.int32, (nd, lanes), 1)
    sub = lax.broadcasted_iota(jnp.int32, (nd, lanes), 0)
    y_all = n_y * cy_len
    x_row = lanes // y_all
    xm, ys = lane // y_all, lane % y_all
    xs = sub * x_row + xm
    slot = ys // cy_len - sub % n_y
    lane8 = lax.broadcasted_iota(jnp.int32, (cx_len, lanes), 1)
    row8 = lax.broadcasted_iota(jnp.int32, (cx_len, lanes), 0)
    lat = jnp.zeros((cx_len, lanes), F32)
    for y in range(cy_len):
        lat = jnp.where(lane8 % cy_len == y, lat_ref[:, y : y + 1], lat)
    lane_x = lane8 // cy_len % n_y * x_row + lane8 // y_all
    lat = jnp.sum(jnp.where(lane_x == row8, lat, 0.0), axis=0, keepdims=True)

    def rows_of(ref):
        v = ref[...].reshape(n_y, x_row, cy_len, cz_len)
        v = jnp.stack([v[:, i] for i in range(x_row)])
        return v.reshape(lanes, cz_len).T

    coef = jnp.exp(rows_of(logc_ref) + lat)
    src = rows_of(source_ref)
    state = rows_of(state_ref)
    for i, v in enumerate((coef, src, state)):
        ext[i, SEND : SEND + cz_len, :] = v
        stage[0, i] = v[cz_len - SEND :]
        stage[1, i] = v[:SEND]
    line = owners_ref[0]
    flags = []
    for j in range(SEND):
        if 0 < j < n_z:
            same = jnp.broadcast_to(line[:, j : j + 1], (1, lanes)) == jnp.broadcast_to(
                line[:, j - 1 : j], (1, lanes)
            )
            flags.append(jnp.where(same, 1.0, 0.0))
        else:
            flags.append(jnp.zeros((1, lanes), F32))
    flags = jnp.concatenate(flags, axis=0)
    for j in range(0, cz_len + 2 * SEND, SEND):
        ext[3, j : j + SEND, :] = flags
    pl.semaphore_wait(barrier, len(greeted))

    def copy(src_at, dst_at, ssem, rsem, device):
        c = pltpu.make_async_remote_copy(
            src_ref=src_at, dst_ref=dst_at, send_sem=ssem, recv_sem=rsem,
            device_id=device, device_id_type=MESH,
        )
        c.start()
        return c

    ends = [
        copy(stage.at[0], ext.at[pl.ds(0, 3), pl.ds(0, SEND)], z_send.at[0], z_recv.at[0],
             (gx, gy, up)),
        copy(stage.at[1], ext.at[pl.ds(0, 3), pl.ds(SEND + cz_len, SEND)],
             z_send.at[1], z_recv.at[1], (gx, gy, down)),
    ]
    for c in ends:
        c.wait()

    def window(first, part):
        at = pl.multiple_of(part * own_n, 8)
        return ext.at[pl.ds(first, 2), pl.ds(at, WIN)]

    main, states = [], []
    for first, group_of, ssem, rsem in (
        (0, main, main_send, main_recv), (2, states, st_send, st_recv),
    ):
        for k in range(1, nd):
            part_of = lax.rem(lax.rem(me + k, nd), parts_n)
            group_of.append(copy(window(first, part_of), gath.at[me, pl.ds(first, 2)],
                                 ssem.at[k], rsem.at[k], place(k, gz)))
    gath[me] = ext[:, pl.ds(pl.multiple_of(mine * own_n, 8), WIN), :]

    def roll(v, shift, axis):
        return pltpu.roll(v, shift % v.shape[axis], axis)

    nx_all = n_x * cx_len

    def masks(s):
        ends_x = jnp.where(xs < s, 1.0, 0.0) + jnp.where(xs >= nx_all - s, 1.0, 0.0)
        ends_y = jnp.where(ys < s, 1.0, 0.0) + jnp.where(ys >= y_all - s, 1.0, 0.0)
        return dict(
            s=s, xhi=(xm >= x_row - s)[None], xlo=(xm < s)[None],
            xin=jnp.where(xs >= nx_all - s, 0.0, 0.5)[None],
            yin=jnp.where(ys >= y_all - s, 0.0, 0.5)[None],
            edge=(ends_x + ends_y)[None],
            xbit=(xs // s % 2 == 0)[None], ybit=(ys // s % 2 == 0)[None],
        )

    def pick(mask, a, b):
        return jnp.where(jnp.broadcast_to(mask, a.shape), a, b)

    def x_next(v, m, row=None):
        s = m["s"]
        if s >= x_row:
            return roll(v, -(s // x_row), 1)
        row = roll(v, -1, 1) if row is None else row
        return roll(pick(m["xlo"], row, v), -s * y_all, 2)

    def x_prev(v, m, row=None):
        s = m["s"]
        if s >= x_row:
            return roll(v, s // x_row, 1)
        row = roll(v, 1, 1) if row is None else row
        return roll(pick(m["xhi"], row, v), s * y_all, 2)

    def y_next(v, m):
        return roll(v, -m["s"], 2)

    def y_prev(v, m):
        return roll(v, m["s"], 2)

    def block_mean(pair, m):
        s = m["s"]
        v = pair + pick(m["ybit"], roll(pair, -s, 2), roll(pair, s, 2))
        if s >= x_row:
            near, far = roll(v, -(s // x_row), 1), roll(v, s // x_row, 1)
        else:
            near, far = roll(v, -s * y_all, 2), roll(v, s * y_all, 2)
        return 0.125 * (v + pick(m["xbit"], near, far))

    def to_plane(v):
        out = v
        for shift in range(1 - n_y, n_y):
            if shift:
                moved = roll(roll(v, -shift, 1), shift * cy_len, 2)
                out = pick((slot == shift)[None], moved, out)
        return out

    m0, m1, m2 = masks(1), masks(2), masks(4)
    first_dev = (gz == 0) & (mine == 0)
    last_dev = (gz == n_z - 1) & (mine == parts_n - 1)
    zero_plane = jnp.zeros((1, nd, lanes), F32)

    def chunks(start, stop, body, step=12):
        for k in range(start, stop, step):
            body(k, min(step, stop - k))

    def pads(ref):
        ref[0:1] = zero_plane
        ref[ref.shape[0] - 1 :] = zero_plane

    for ref in (va, vb, ma, mb):
        pads(ref)

    def level(c, length, halo, own, scale, m, xr, wr, yr, zr, dr, ir):
        half = 0.5 * scale * ANISO
        c[0:1], c[length + 1 :] = c[1:2], c[length : length + 1]
        lo, hi = halo, halo + own + 1
        c[lo : lo + 1] = jnp.where(first_dev, c[lo + 1 : lo + 2], c[lo : lo + 1])
        c[hi : hi + 1] = jnp.where(last_dev, c[hi - 1 : hi], c[hi : hi + 1])

        def body(k, n):
            here = c[pl.ds(k + 1, n)]
            wz = half * (c[pl.ds(k, n)] + here)
            zr[pl.ds(k, n)] = wz
            wx = (scale * m["xin"]) * (here + x_next(here, m))
            wy = (scale * m["yin"]) * (here + y_next(here, m))
            wp = x_prev(wx, m)
            diag = wx + wp + wy + y_prev(wy, m) + (scale * m["edge"]) * here
            diag = diag + wz + half * (c[pl.ds(k + 2, n)] + here)
            dr[pl.ds(k, n)] = diag
            if xr is not None:
                xr[pl.ds(k, n)] = wx
                wr[pl.ds(k, n)] = wp
                yr[pl.ds(k, n)] = wy
                ir[pl.ds(k, n)] = OMEGA / diag

        chunks(0, length, body)
        zr[0:1] = zero_plane
        zr[length : length + 1] = zero_plane
        lo, hi = halo, halo + own
        zr[lo : lo + 1] = jnp.where(first_dev, 0.0, zr[lo : lo + 1])
        zr[hi : hi + 1] = jnp.where(last_dev, 0.0, zr[hi : hi + 1])

    def pull(v, k, n, m, xr, wr, yr, zr):
        near, wz = v[pl.ds(k, n + 2)], zr[pl.ds(k, n + 1)]
        here = near[1 : n + 1]
        if m["s"] < x_row:
            rows = v.reshape(v.shape[0] * nd, lanes)
            later = rows[pl.ds((k + 1) * nd + 1, n * nd), :].reshape(n, nd, lanes)
            prior = rows[pl.ds((k + 1) * nd - 1, n * nd), :].reshape(n, nd, lanes)
        else:
            later = prior = None
        wy = yr[pl.ds(k, n)]
        total = wz[:n] * near[:n] + wz[1:] * near[2:]
        total = total + (wy * y_next(here, m) + y_prev(wy * here, m))
        total = total + xr[pl.ds(k, n)] * x_next(here, m, later)
        total = total + wr[pl.ds(k, n)] * x_prev(here, m, prior)
        return here, total

    def sweep(v, out, b, start, stop, m, xr, wr, yr, zr, ir):
        def body(k, n):
            here, total = pull(v, k, n, m, xr, wr, yr, zr)
            out[pl.ds(k + 1, n)] = (1.0 - OMEGA) * here + ir[pl.ds(k, n)] * (
                b[pl.ds(k, n)] + total)
        chunks(start, stop, body)

    fine = (m0, x0, w0, y0, z0)
    mid = (m1, x1, w1, y1, z1)

    for c in main:
        c.wait()
    flat = gath.reshape(nd * 4 * WIN, lanes)

    def planes(which, start, n):
        return to_plane(jnp.stack([
            flat[pl.ds(which * WIN + start + u, nd, stride=4 * WIN), :] for u in range(n)]))

    def spread(k, n):
        c0[pl.ds(1 + k, n)] = planes(0, SEND - HALO + k, n)
        b0[pl.ds(k, n)] = planes(1, SEND - HALO + k, n)

    chunks(0, Z0, spread)

    def pairs(ref, k, step):
        v = ref[pl.ds(k, 2 * step)].reshape(step, 2, nd, lanes)
        return v[:, 0] + v[:, 1]

    def coarsen1(K, n):
        c1[pl.ds(K + 1, n)] = block_mean(pairs(c0, 1 + 2 * K, n), m0)

    chunks(0, Z1, coarsen1)

    def coarsen2(K, n):
        c2[pl.ds(K + 1, n)] = block_mean(pairs(c1, 1 + H1 - 2 + 2 * K, n), m1)

    chunks(0, Z2, coarsen2)
    level(c0, Z0, HALO, own_n, 1.0, m0, x0, w0, y0, z0, d0, i0)
    level(c1, Z1, H1, L1, 0.25, m1, x1, w1, y1, z1, d1, i1)
    level(c2, Z2, 1, L2, 0.0625, m2, None, None, None, z2, d2, None)

    low[mine, 0] = d2[1 : 1 + L2]
    low[mine, 1] = z2[1 : 1 + L2]
    lows = []
    for k in range(1, parts_n):
        lows.append(copy(low.at[mine], low.at[mine], low_send.at[k], low_recv.at[k], member(k)[1]))

    def first0(k, n):
        va[pl.ds(k + 1, n)] = i0[pl.ds(k, n)] * b0[pl.ds(k, n)]

    chunks(0, Z0, first0)
    sweep(va, vb, b0, 1, Z0 - 1, *fine, i0)
    sweep(vb, va, b0, 2, Z0 - 2, *fine, i0)

    def residual(v, b, d, k, n, m, *weights):
        here, total = pull(v, k, 2 * n, m, *weights)
        r = b[pl.ds(k, 2 * n)] + total - d[pl.ds(k, 2 * n)] * here
        r = r.reshape(n, 2, nd, lanes)
        return block_mean(r[:, 0] + r[:, 1], m)

    def resid0(K, n):
        b1[pl.ds(K, n)] = residual(va, b0, d0, 2 * K, n, *fine)

    chunks(2, Z1 - 2, resid0, 8)

    def first1(k, n):
        ma[pl.ds(k + 1, n)] = i1[pl.ds(k, n)] * b1[pl.ds(k, n)]

    chunks(2, Z1 - 2, first1)
    sweep(ma, mb, b1, 3, Z1 - 3, *mid, i1)
    sweep(mb, ma, b1, 4, Z1 - 4, *mid, i1)

    mids = [
        copy(ma.at[pl.ds(1 + L1, H1)], mid_lo.at[0], mid_send.at[0], mid_recv.at[0], along(1)),
        copy(b1.at[pl.ds(L1, H1)], mid_lo.at[1], mid_send.at[1], mid_recv.at[1], along(1)),
        copy(ma.at[pl.ds(1 + H1, H1)], mid_hi.at[0], mid_send.at[2], mid_recv.at[2], along(-1)),
        copy(b1.at[pl.ds(H1, H1)], mid_hi.at[1], mid_send.at[3], mid_recv.at[3], along(-1)),
    ]

    rlow[mine] = residual(ma, b1, d1, H1, L2, *mid)
    rights = []
    for k in range(1, parts_n):
        rights.append(copy(rlow.at[mine], rlow.at[mine], r_send.at[k], r_recv.at[k], member(k)[1]))
    for c in lows:
        c.wait()

    def dk(k):
        return low[k // L2, 0, k % L2]

    def ek(k):
        return low[k // L2, 1, k % L2]

    inv = 1.0 / dk(0)
    fac[2, 0] = inv
    p_now = jnp.ones((nd, lanes), F32)
    forward_p = [p_now]
    for k in range(1, NL):
        e = ek(k)
        t = e * inv
        fac[1, k - 1] = t
        inv = 1.0 / (dk(k) - e * t)
        p_now = t * p_now
        fac[0, k], fac[2, k] = t, inv
        spike[1, k] = p_now
    spike[1, 0] = forward_p[0]
    p, q = p_now * inv, inv
    spike[1, NL - 1], spike[2, NL - 1] = p, q
    last_p, last_q = p, q
    for k in range(NL - 2, -1, -1):
        f = fac[1, k]
        p = spike[1, k] * fac[2, k] + f * p
        q = f * q
        spike[1, k], spike[2, k] = p, q
    for c in states:
        c.wait()
    cut_plane = planes(3, gz, 1)[0]
    for c in rights:
        c.wait()
    y = rlow[0, 0]
    spike[0, 0] = y
    for k in range(1, NL):
        y = rlow[k // L2, k % L2] + fac[0, k] * y
        spike[0, k] = y
    g = y * fac[2, NL - 1]
    spike[0, NL - 1] = g
    last_g = g
    for k in range(NL - 2, -1, -1):
        g = spike[0, k] * fac[2, k] + fac[1, k] * g
        spike[0, k] = g
    for i, (a, b) in enumerate(((g, last_g), (p, last_p), (q, last_q))):
        iface[gz, i], iface[gz, 3 + i] = a, b
    iface[gz, 6] = ek(0) * cut_plane
    ifs = []
    for j in range(1, n_z):
        ifs.append(copy(iface.at[gz], iface.at[gz], if_send.at[j], if_recv.at[j],
                        (gx, gy, lax.rem(gz + j, n_z))))
    ifs.append(copy(spike.at[:, pl.ds(NL - 3, 3)], spk_lo, if_send.at[n_z], if_recv.at[n_z],
                    (gx, gy, up)))
    ifs.append(copy(spike.at[:, pl.ds(0, 3)], spk_hi, if_send.at[n_z + 1], if_recv.at[n_z + 1],
                    (gx, gy, down)))

    s0[...] = planes(2, SEND - 1, own_n + 2)
    s0[0:1] = jnp.where(first_dev, 0.0, s0[0:1])
    s0[own_n + 1 :] = jnp.where(last_dev, 0.0, s0[own_n + 1 :])

    for c in mids + ifs:
        c.wait()

    zero = jnp.zeros((nd, lanes), F32)
    A, B = zero, zero
    kept = []
    for j in range(n_z):
        c = iface[j, 6]
        g, p, q = iface[j, 0], iface[j, 1], iface[j, 2]
        gl, plast, ql = iface[j, 3], iface[j, 4], iface[j, 5]
        inv = 1.0 / (1.0 - p * c * B)
        F = (g + p * c * A) * inv
        G = q * inv
        kept.append((c, A, B, F, G))
        nxt = iface[j + 1, 6] if j + 1 < n_z else zero
        tail = plast * c
        A, B = gl + tail * (A + B * F), (ql + tail * B * G) * nxt
    right = zero
    for j in reversed(range(n_z)):
        c, A, B, F, G = kept[j]
        head = F + G * right
        sides[j, 0] = c * (A + B * head)
        sides[j, 1] = right
        right = c * head

    L, R = sides[gz, 0], sides[gz, 1]

    def twice(v):
        return jnp.broadcast_to(v[:, None], (v.shape[0], 2, nd, lanes)).reshape(
            2 * v.shape[0], nd, lanes)

    corr[3 : 3 + NL] = spike[0] + spike[1] * L + spike[2] * R
    corr[0:3] = spk_lo[0] + spk_lo[1] * sides[down, 0] + spk_lo[2] * sides[down, 1]
    corr[3 + NL :] = spk_hi[0] + spk_hi[1] * sides[up, 0] + spk_hi[2] * sides[up, 1]
    near = twice(corr[pl.ds(mine * L2, L2 + 6)])
    ma[1 : 1 + H1] = mid_lo[0]
    ma[1 + H1 + L1 : 1 + 2 * H1 + L1] = mid_hi[0]
    ma[1 : 1 + Z1] = ma[1 : 1 + Z1] + near[6 - H1 : 6 - H1 + Z1]
    b1[0:H1] = mid_lo[1]
    b1[H1 + L1 :] = mid_hi[1]

    sweep(ma, mb, b1, 1, Z1 - 1, *mid, i1)
    sweep(mb, ma, b1, 2, Z1 - 2, *mid, i1)
    sweep(ma, mb, b1, 3, Z1 - 3, *mid, i1)

    def raise0(K, n):
        k = 1 + 2 * K
        va[pl.ds(k, 2 * n)] = va[pl.ds(k, 2 * n)] + twice(mb[pl.ds(K + 1, n)])

    chunks(3, Z1 - 3, raise0, 8)
    sweep(va, vb, b0, HALO - 3, HALO + own_n + 3, *fine, i0)
    sweep(vb, va, b0, HALO - 2, HALO + own_n + 2, *fine, i0)
    sweep(va, vb, b0, HALO - 1, HALO + own_n + 1, *fine, i0)

    lo, hi = HALO, HALO + own_n + 1
    vb[lo : lo + 1] = jnp.where(first_dev, -vb[lo + 1 : lo + 2], vb[lo : lo + 1])
    vb[hi : hi + 1] = jnp.where(last_dev, -vb[hi - 1 : hi], vb[hi : hi + 1])

    def terms(i, n):
        a, s = vb[pl.ds(HALO + 1 + i, n)], s0[pl.ds(1 + i, n)]
        tx = m0["xin"] * ((a - x_next(a, m0)) * (s - x_next(s, m0)))
        ty = m0["yin"] * ((a - y_next(a, m0)) * (s - y_next(s, m0)))
        t = tx + x_prev(tx, m0) + ty + y_prev(ty, m0) + m0["edge"] * (a * s)
        z = (a - vb[pl.ds(HALO + i, n)]) * (s - s0[pl.ds(i, n)])
        z = z + (a - vb[pl.ds(HALO + 2 + i, n)]) * (s - s0[pl.ds(2 + i, n)])
        return jnp.sum(c0[pl.ds(HALO + 1 + i, n)] * (t + 0.5 * z), axis=0)

    acc = terms(0, own_n)

    vb[HALO + 1 : HALO + 1 + own_n] = to_plane(vb[HALO + 1 : HALO + 1 + own_n])
    va[0] = to_plane(acc[None])[0]
    vflat = vb.reshape(vb.shape[0] * nd, lanes)
    for d in range(nd):
        outs[d, 0:own_n, :] = vflat[pl.ds((HALO + 1) * nd + d, own_n, stride=nd), :]
        outs[d, own_n:, :] = jnp.broadcast_to(va[0, d : d + 1, :], (8, lanes))
    fins = []
    for k in range(1, parts_n):
        peer, device = member(k)
        fins.append(copy(outs.at[peer], fin.at[mine], fin_send.at[k], fin_recv.at[k], device))
    fin[mine] = outs[me]
    for c in fins:
        c.wait()
    sums = fin[0, own_n:, :]
    for i in range(1, parts_n):
        sums = sums + fin[i, own_n:, :]
    part[gz] = sums
    parts = []
    for j in range(1, n_z):
        parts.append(copy(part.at[gz], part.at[gz], pt_send.at[j], pt_recv.at[j],
                          (gx, gy, lax.rem(gz + j, n_z))))
    field = fin[:, 0:own_n, :].reshape(cz_len, lanes).T.reshape(x_row, n_y, cy_len, cz_len)
    for a in range(n_y):
        for i in range(x_row):
            adj_ref[a * x_row + i] = field[i, a]

    for c in parts:
        c.wait()
    total = part[0]
    for j in range(1, n_z):
        total = total + part[j]
    rows = total[0:cx_len] * (-1.0 / math.sqrt(n_total))
    width = cy_len // n_z
    for j in range(width):
        here = lane8 == row8 % x_row * y_all + row8 // x_row * cy_len + gz * width + j
        grad_ref[:, j : j + 1] = jnp.sum(jnp.where(here, rows, 0.0), axis=1, keepdims=True)


def solution(mesh):
    n_x, n_y, n_z = mesh.shape["gx"], mesh.shape["gy"], mesh.shape["gz"]
    nd = n_x * n_y

    def per_device(source, state, log_coef, lateral, owners):
        cx, cy, cz = source.shape
        lanes = cx * cy
        parts_n = min(nd, 8)
        own = cz // parts_n
        Z0, Z1, Z2, H1 = own + 2 * HALO, own // 2 + HALO, own // 4 + 2, HALO // 2
        L2, NL = own // 4, cz // 4
        V = lambda *shape: pltpu.VMEM(shape, F32)
        pln = lambda k: V(k, nd, lanes)
        D = lambda k: pltpu.SemaphoreType.DMA((k,))
        vm = pl.BlockSpec(memory_space=pltpu.VMEM)
        return pl.pallas_call(
            functools.partial(kernel, n_x, n_y, n_z, cx, cy, cz, cz * n_z),
            out_shape=(
                jax.ShapeDtypeStruct((cx, cy, cz), F32),
                jax.ShapeDtypeStruct((cx, cy // n_z), F32),
            ),
            in_specs=[vm] * 5,
            out_specs=(vm, vm),
            scratch_shapes=[
                V(4, cz + 2 * SEND, lanes), V(2, 3, SEND, lanes),
                V(nd, 4, own + 2 * SEND, lanes),
                pln(Z0 + 2), pln(Z0), pln(Z0), pln(Z0), pln(Z0 + 1), pln(Z0), pln(Z0), pln(Z0),
                pln(Z0 + 2), pln(Z0 + 2),
                pln(Z1 + 2), pln(Z1), pln(Z1), pln(Z1), pln(Z1 + 1), pln(Z1), pln(Z1), pln(Z1),
                pln(Z1 + 2), pln(Z1 + 2),
                pln(Z2 + 2), pln(Z2 + 1), pln(Z2),
                V(parts_n, 2, L2, nd, lanes), V(parts_n, L2, nd, lanes),
                V(3, NL, nd, lanes), V(3, NL, nd, lanes), pln(NL + 6),
                pln(own + 2), V(n_z, 7, nd, lanes), V(n_z, 2, nd, lanes),
                V(2, H1, nd, lanes), V(2, H1, nd, lanes),
                V(3, 3, nd, lanes), V(3, 3, nd, lanes),
                V(nd, own + 8, lanes), V(parts_n, own + 8, lanes), V(n_z, 8, lanes),
                D(2), D(2), D(nd), D(nd), D(nd), D(nd),
                D(nd), D(nd), D(nd), D(nd),
                D(4), D(4), D(n_z + 2), D(n_z + 2), D(nd), D(nd), D(n_z), D(n_z),
            ],
            compiler_params=pltpu.CompilerParams(
                collective_id=0, has_side_effects=True, vmem_limit_bytes=56 * 1024 * 1024
            ),
            cost_estimate=pl.CostEstimate(
                flops=100_000_000, bytes_accessed=400_000, transcendentals=20_000
            ),
        )(source, state, log_coef, lateral, owners)

    placed = (
        P("gx", "gy", "gz"),
        P("gx", "gy", "gz"),
        P("gx", "gy", "gz"),
        P("gx", "gy"),
        P("gx", "gy", None),
    )
    return jax.shard_map(
        per_device,
        mesh=mesh,
        in_specs=placed,
        out_specs=(P("gx", "gy", "gz"), P("gx", ("gy", "gz"))),
        check_vma=False,
    )
```

time: 57.9 us -> 45.2 us (0.78)
  Pallas kernels: 54.2 us -> 41.6 us
    pallas_call x1, Pallas kernels: 54.2 us -> 41.6 us  [per_device(): pl.pallas_call(functools.partial(kernel, n_x, n_y, n_z, cx, cy, cz, cz *...]
where the time goes in v4:
time: 45.2 us; the launch traced here: 45 us
  Pallas kernels  41.6 us (92%)
  local copies, waits for them, and re-layouts  2.8 us (6%)
  between operations  0.64 us (1%)
    pallas_call x1, Pallas kernels, per_device(): pl.pallas_call(functools.partial(kernel, n_x, n_y, n_z, cx, cy, cz, cz *...  41.6 us
    unnamed x1, local copies, waits for them, and re-layouts  1.47 us
    pallas_call x1, local copies, waits for them, and re-layouts, per_device(): pl.pallas_call(functools.partial(kernel, n_x, n_y, n_z, cx, cy, cz, cz *...  1.33 us

profile of v4, /device:TPU:0, one launch (start us, length us, event | category | flops | bytes accessed | tf_op | source)
XLA Modules:
  0.0 45.0 jit_solution(5595671555579200312)
XLA Ops:
  0.6 41.6 %shard_map.68 = (f32[8,16,128]{2,1,0:T(8,128)}, f32[8,4]{1,0:T(8,128)}) custom-call(f32[8,16,128]{2,1,0:T(8,128)} %source_ref.1, f32[8,16,128]{2,1,0:T(8,128)} %state_ref.1, f32[8,16,128]{2,1,0:T(8,128)} %logc_ref.1, f32[8,16]{1,0:T(8,128)} %lat_ref.1, s32[1,1,4]{2,1,0:T(1,128)} %owners_ref.1), custom_call_target="tpu_custom_call" | custom-call | flops 100000000 | bytes 400000 | tf_op jit(solution)/shard_map/pallas_call | solution.py:524
  42.2 1.3 %copy.7 = f32[8,4]{0,1:T(4,128)} copy(f32[8,4]{1,0:T(8,128)} %get-tuple-element.3) | data formatting | bytes 256 | tf_op jit(solution)/shard_map/pallas_call | solution.py:524
  43.5 1.5 %copy.9 = f32[8,16,128]{2,1,0:T(8,128)} copy(f32[8,16,128]{2,1,0:T(8,128)} %get-tuple-element.6) | data formatting | bytes 131072

commit v5 on v4

--- a/solution.py
+++ b/solution.py
@@ -20,7 +20,7 @@
     n_x, n_y, n_z, cx_len, cy_len, cz_len, n_total,
     source_ref, state_ref, logc_ref, lat_ref, owners_ref,
     adj_ref, grad_ref,
-    ext, stage, gath,
+    ext, gath,
     c0, x0, w0, y0, z0, d0, i0, b0, va, vb,
     c1, x1, w1, y1, z1, d1, i1, b1, ma, mb,
     c2, z2, d2, low, rlow, fac, spike, corr,
@@ -60,8 +60,15 @@
     greeted = [place(k, gz) for k in range(1, nd)]
     greeted += [(gx, gy, lax.rem(gz + j, n_z)) for j in range(1, n_z)]
     greeted += [along(1), along(-1)]
-    for device in greeted:
-        pl.semaphore_signal(barrier, inc=1, device_id=device, device_id_type=MESH)
+    groups = nd // parts_n
+
+    def greet(devices):
+        for device in devices:
+            pl.semaphore_signal(barrier, inc=1, device_id=device, device_id_type=MESH)
+
+    greet(greeted)
+    pl.when(mine == 0)(lambda: greet([place(k, down) for k in range(nd)]))
+    pl.when(mine == parts_n - 1)(lambda: greet([place(k, up) for k in range(nd)]))
 
     lane = lax.broadcasted_iota(jnp.int32, (nd, lanes), 1)
     sub = lax.broadcasted_iota(jnp.int32, (nd, lanes), 0)
@@ -85,11 +92,66 @@
 
     coef = jnp.exp(rows_of(logc_ref) + lat)
     src = rows_of(source_ref)
-    state = rows_of(state_ref)
-    for i, v in enumerate((coef, src, state)):
+    for i, v in enumerate((coef, src)):
         ext[i, SEND : SEND + cz_len, :] = v
-        stage[0, i] = v[cz_len - SEND :]
-        stage[1, i] = v[:SEND]
+        ext[i, 0:SEND, :] = jnp.zeros((SEND, lanes), F32)
+        ext[i, SEND + cz_len :, :] = jnp.zeros((SEND, lanes), F32)
+    pl.semaphore_wait(barrier, len(greeted) + 2 * groups)
+
+    def copy(src_at, dst_at, ssem, rsem, device):
+        c = pltpu.make_async_remote_copy(
+            src_ref=src_at, dst_ref=dst_at, send_sem=ssem, recv_sem=rsem,
+            device_id=device, device_id_type=MESH,
+        )
+        c.start()
+        return c
+
+    def window(first, part):
+        at = pl.multiple_of(part * own_n, 8)
+        return ext.at[pl.ds(first, 2), pl.ds(at, WIN)]
+
+    def deal(first, ssem, rsem):
+        sent = []
+        for k in range(1, nd):
+            part_of = lax.rem(lax.rem(me + k, nd), parts_n)
+            sent.append(copy(window(first, part_of), gath.at[me, pl.ds(first, 2), pl.ds(0, WIN)],
+                             ssem.at[k], rsem.at[k], place(k, gz)))
+        return sent
+
+    def beyond(first, at):
+        sent = []
+        for i in range(groups):
+            for end, row, z, to in (
+                (0, cz_len, up, i * parts_n), (1, SEND, down, (i + 1) * parts_n - 1),
+            ):
+                sent.append(copy(
+                    ext.at[pl.ds(first, 2), pl.ds(row, SEND)],
+                    gath.at[me, pl.ds(first, 2), pl.ds(WIN + end * SEND, SEND)],
+                    z_send.at[at + 2 * i + end], z_recv.at[at * nd // 2 // groups + me],
+                    (to // n_y, to % n_y, z)))
+        return sent
+
+    def beyond_wait(first, at, sent):
+        for c in sent:
+            c.wait_send()
+
+        def arrive(end):
+            for d in range(nd):
+                pltpu.make_async_remote_copy(
+                    src_ref=ext.at[pl.ds(first, 2), pl.ds(0, SEND)],
+                    dst_ref=gath.at[d, pl.ds(first, 2), pl.ds(WIN + end * SEND, SEND)],
+                    send_sem=z_send.at[0], recv_sem=z_recv.at[at * nd // 2 // groups + d],
+                    device_id=place(1, gz), device_id_type=MESH,
+                ).wait_recv()
+
+        pl.when(mine == 0)(lambda: arrive(0))
+        pl.when(mine == parts_n - 1)(lambda: arrive(1))
+
+    main = deal(0, main_send, main_recv)
+    main_z = beyond(0, 0)
+    ext[2, SEND : SEND + cz_len, :] = rows_of(state_ref)
+    ext[2, 0:SEND, :] = jnp.zeros((SEND, lanes), F32)
+    ext[2, SEND + cz_len :, :] = jnp.zeros((SEND, lanes), F32)
     line = owners_ref[0]
     flags = []
     for j in range(SEND):
@@ -103,38 +165,12 @@
     flags = jnp.concatenate(flags, axis=0)
     for j in range(0, cz_len + 2 * SEND, SEND):
         ext[3, j : j + SEND, :] = flags
-    pl.semaphore_wait(barrier, len(greeted))
-
-    def copy(src_at, dst_at, ssem, rsem, device):
-        c = pltpu.make_async_remote_copy(
-            src_ref=src_at, dst_ref=dst_at, send_sem=ssem, recv_sem=rsem,
-            device_id=device, device_id_type=MESH,
-        )
-        c.start()
-        return c
-
-    ends = [
-        copy(stage.at[0], ext.at[pl.ds(0, 3), pl.ds(0, SEND)], z_send.at[0], z_recv.at[0],
-             (gx, gy, up)),
-        copy(stage.at[1], ext.at[pl.ds(0, 3), pl.ds(SEND + cz_len, SEND)],
-             z_send.at[1], z_recv.at[1], (gx, gy, down)),
-    ]
-    for c in ends:
-        c.wait()
-
-    def window(first, part):
-        at = pl.multiple_of(part * own_n, 8)
-        return ext.at[pl.ds(first, 2), pl.ds(at, WIN)]
-
-    main, states = [], []
-    for first, group_of, ssem, rsem in (
-        (0, main, main_send, main_recv), (2, states, st_send, st_recv),
-    ):
-        for k in range(1, nd):
-            part_of = lax.rem(lax.rem(me + k, nd), parts_n)
-            group_of.append(copy(window(first, part_of), gath.at[me, pl.ds(first, 2)],
-                                 ssem.at[k], rsem.at[k], place(k, gz)))
-    gath[me] = ext[:, pl.ds(pl.multiple_of(mine * own_n, 8), WIN), :]
+    states = deal(2, st_send, st_recv)
+    states_z = beyond(2, 2 * groups)
+    gath[me, :, 0:WIN, :] = ext[:, pl.ds(pl.multiple_of(mine * own_n, 8), WIN), :]
+    from_lo = (parts_n - 1 - mine) // (parts_n - 1) * WIN
+    from_hi = mine // (parts_n - 1) * (2 * SEND)
+    HIGH = WIN + 2 * SEND
 
     def roll(v, shift, axis):
         return pltpu.roll(v, shift % v.shape[axis], axis)
@@ -266,17 +302,22 @@
 
     for c in main:
         c.wait()
-    flat = gath.reshape(nd * 4 * WIN, lanes)
+    beyond_wait(0, 0, main_z)
+    flat = gath.reshape(nd * 4 * HIGH, lanes)
 
     def planes(which, start, n):
         return to_plane(jnp.stack([
-            flat[pl.ds(which * WIN + start + u, nd, stride=4 * WIN), :] for u in range(n)]))
+            flat[pl.ds(which * HIGH + start + u, nd, stride=4 * HIGH), :] for u in range(n)]))
 
     def spread(k, n):
         c0[pl.ds(1 + k, n)] = planes(0, SEND - HALO + k, n)
         b0[pl.ds(k, n)] = planes(1, SEND - HALO + k, n)
 
-    chunks(0, Z0, spread)
+    chunks(HALO, HALO + own_n, spread)
+    for which, ref, pad in ((0, c0, 1), (1, b0, 0)):
+        ref[pad : pad + HALO] = planes(which, from_lo + SEND - HALO, HALO)
+        hi = pad + HALO + own_n
+        ref[hi : hi + HALO] = planes(which, from_hi + SEND + own_n, HALO)
 
     def pairs(ref, k, step):
         v = ref[pl.ds(k, 2 * step)].reshape(step, 2, nd, lanes)
@@ -369,7 +410,8 @@
         spike[1, k], spike[2, k] = p, q
     for c in states:
         c.wait()
-    cut_plane = planes(3, gz, 1)[0]
+    beyond_wait(2, 2 * groups, states_z)
+    cut_plane = planes(3, SEND + gz, 1)[0]
     for c in rights:
         c.wait()
     y = rlow[0, 0]
@@ -395,7 +437,9 @@
     ifs.append(copy(spike.at[:, pl.ds(0, 3)], spk_hi, if_send.at[n_z + 1], if_recv.at[n_z + 1],
                     (gx, gy, down)))
 
-    s0[...] = planes(2, SEND - 1, own_n + 2)
+    s0[1 : own_n + 1] = planes(2, SEND, own_n)
+    s0[0:1] = planes(2, from_lo + SEND - 1, 1)
+    s0[own_n + 1 :] = planes(2, from_hi + SEND + own_n, 1)
     s0[0:1] = jnp.where(first_dev, 0.0, s0[0:1])
     s0[own_n + 1 :] = jnp.where(last_dev, 0.0, s0[own_n + 1 :])
 
@@ -530,8 +574,8 @@
             in_specs=[vm] * 5,
             out_specs=(vm, vm),
             scratch_shapes=[
-                V(4, cz + 2 * SEND, lanes), V(2, 3, SEND, lanes),
-                V(nd, 4, own + 2 * SEND, lanes),
+                V(4, cz + 2 * SEND, lanes),
+                V(nd, 4, own + 4 * SEND, lanes),
                 pln(Z0 + 2), pln(Z0), pln(Z0), pln(Z0), pln(Z0 + 1), pln(Z0), pln(Z0), pln(Z0),
                 pln(Z0 + 2), pln(Z0 + 2),
                 pln(Z1 + 2), pln(Z1), pln(Z1), pln(Z1), pln(Z1 + 1), pln(Z1), pln(Z1), pln(Z1),
@@ -543,7 +587,7 @@
                 V(2, H1, nd, lanes), V(2, H1, nd, lanes),
                 V(3, 3, nd, lanes), V(3, 3, nd, lanes),
                 V(nd, own + 8, lanes), V(parts_n, own + 8, lanes), V(n_z, 8, lanes),
-                D(2), D(2), D(nd), D(nd), D(nd), D(nd),
+                D(4 * nd // parts_n), D(2 * nd), D(nd), D(nd), D(nd), D(nd),
                 D(nd), D(nd), D(nd), D(nd),
                 D(4), D(4), D(n_z + 2), D(n_z + 2), D(nd), D(nd), D(n_z), D(n_z),
             ],

time: 45.2 us -> 44.2 us (0.978)
  Pallas kernels: 41.6 us -> 40.6 us
    pallas_call x1, Pallas kernels: 41.6 us -> 40.6 us  [per_device(): pl.pallas_call(functools.partial(kernel, n_x, n_y, n_z, cx, cy, cz, cz *...]
where the time goes in v5:
time: 44.2 us; the launch traced here: 44 us
  Pallas kernels  40.6 us (92%)
  local copies, waits for them, and re-layouts  2.8 us (6%)
  between operations  0.64 us (1%)
    pallas_call x1, Pallas kernels, per_device(): pl.pallas_call(functools.partial(kernel, n_x, n_y, n_z, cx, cy, cz, cz *...  40.6 us
    unnamed x1, local copies, waits for them, and re-layouts  1.47 us
    pallas_call x1, local copies, waits for them, and re-layouts, per_device(): pl.pallas_call(functools.partial(kernel, n_x, n_y, n_z, cx, cy, cz, cz *...  1.33 us

profile of v5, /device:TPU:0, one launch (start us, length us, event | category | flops | bytes accessed | tf_op | source)
XLA Modules:
  0.0 44.0 jit_solution(11683234765753013861)
XLA Ops:
  0.6 40.6 %shard_map.68 = (f32[8,16,128]{2,1,0:T(8,128)}, f32[8,4]{1,0:T(8,128)}) custom-call(f32[8,16,128]{2,1,0:T(8,128)} %source_ref.1, f32[8,16,128]{2,1,0:T(8,128)} %state_ref.1, f32[8,16,128]{2,1,0:T(8,128)} %logc_ref.1, f32[8,16]{1,0:T(8,128)} %lat_ref.1, s32[1,1,4]{2,1,0:T(1,128)} %owners_ref.1), custom_call_target="tpu_custom_call" | custom-call | flops 100000000 | bytes 400000 | tf_op jit(solution)/shard_map/pallas_call | solution.py:568
  41.2 1.3 %copy.7 = f32[8,4]{0,1:T(4,128)} copy(f32[8,4]{1,0:T(8,128)} %get-tuple-element.3) | data formatting | bytes 256 | tf_op jit(solution)/shard_map/pallas_call | solution.py:568
  42.5 1.5 %copy.9 = f32[8,16,128]{2,1,0:T(8,128)} copy(f32[8,16,128]{2,1,0:T(8,128)} %get-tuple-element.6) | data formatting | bytes 131072

commit v6 on v5

--- a/solution.py
+++ b/solution.py
@@ -18,14 +18,14 @@
 
 def kernel(
     n_x, n_y, n_z, cx_len, cy_len, cz_len, n_total,
-    source_ref, state_ref, logc_ref, lat_ref, owners_ref,
+    source_in, state_in, logc_in, lat_ref, owners_ref,
     adj_ref, grad_ref,
-    ext, gath,
+    logc_ref, source_ref, state_ref, in_sem, ext, gath,
     c0, x0, w0, y0, z0, d0, i0, b0, va, vb,
     c1, x1, w1, y1, z1, d1, i1, b1, ma, mb,
     c2, z2, d2, low, rlow, fac, spike, corr,
     s0, iface, sides, mid_lo, mid_hi, spk_lo, spk_hi, outs, fin, part,
-    z_send, z_recv, main_send, main_recv, st_send, st_recv,
+    z_send, z_recv, main_send, main_recv, src_send, src_recv, st_send, st_recv,
     low_send, low_recv, r_send, r_recv,
     mid_send, mid_recv, if_send, if_recv, fin_send, fin_recv, pt_send, pt_recv,
 ):
@@ -56,6 +56,12 @@
         peer = group + lax.rem(t, parts_n)
         return (lax.div(peer, n_y), lax.rem(peer, n_y), lax.div(t, parts_n))
 
+    fetches = []
+    for i, (a, b) in enumerate(
+        ((logc_in, logc_ref), (source_in, source_ref), (state_in, state_ref))
+    ):
+        fetches.append(pltpu.make_async_copy(a, b, in_sem.at[i]))
+        fetches[i].start()
     barrier = pltpu.get_barrier_semaphore()
     greeted = [place(k, gz) for k in range(1, nd)]
     greeted += [(gx, gy, lax.rem(gz + j, n_z)) for j in range(1, n_z)]
@@ -90,7 +96,9 @@
         v = jnp.stack([v[:, i] for i in range(x_row)])
         return v.reshape(lanes, cz_len).T
 
+    fetches[0].wait()
     coef = jnp.exp(rows_of(logc_ref) + lat)
+    fetches[1].wait()
     src = rows_of(source_ref)
     for i, v in enumerate((coef, src)):
         ext[i, SEND : SEND + cz_len, :] = v
@@ -106,15 +114,16 @@
         c.start()
         return c
 
-    def window(first, part):
+    def window(first, count, part):
         at = pl.multiple_of(part * own_n, 8)
-        return ext.at[pl.ds(first, 2), pl.ds(at, WIN)]
-
-    def deal(first, ssem, rsem):
+        return ext.at[pl.ds(first, count), pl.ds(at, WIN)]
+
+    def deal(first, count, ssem, rsem):
         sent = []
         for k in range(1, nd):
             part_of = lax.rem(lax.rem(me + k, nd), parts_n)
-            sent.append(copy(window(first, part_of), gath.at[me, pl.ds(first, 2), pl.ds(0, WIN)],
+            sent.append(copy(window(first, count, part_of),
+                             gath.at[me, pl.ds(first, count), pl.ds(0, WIN)],
                              ssem.at[k], rsem.at[k], place(k, gz)))
         return sent
 
@@ -147,8 +156,10 @@
         pl.when(mine == 0)(lambda: arrive(0))
         pl.when(mine == parts_n - 1)(lambda: arrive(1))
 
-    main = deal(0, main_send, main_recv)
+    main = deal(0, 1, main_send, main_recv)
     main_z = beyond(0, 0)
+    sources = deal(1, 1, src_send, src_recv)
+    fetches[2].wait()
     ext[2, SEND : SEND + cz_len, :] = rows_of(state_ref)
     ext[2, 0:SEND, :] = jnp.zeros((SEND, lanes), F32)
     ext[2, SEND + cz_len :, :] = jnp.zeros((SEND, lanes), F32)
@@ -165,8 +176,6 @@
     flags = jnp.concatenate(flags, axis=0)
     for j in range(0, cz_len + 2 * SEND, SEND):
         ext[3, j : j + SEND, :] = flags
-    states = deal(2, st_send, st_recv)
-    states_z = beyond(2, 2 * groups)
     gath[me, :, 0:WIN, :] = ext[:, pl.ds(pl.multiple_of(mine * own_n, 8), WIN), :]
     from_lo = (parts_n - 1 - mine) // (parts_n - 1) * WIN
     from_hi = mine // (parts_n - 1) * (2 * SEND)
@@ -309,15 +318,16 @@
         return to_plane(jnp.stack([
             flat[pl.ds(which * HIGH + start + u, nd, stride=4 * HIGH), :] for u in range(n)]))
 
-    def spread(k, n):
-        c0[pl.ds(1 + k, n)] = planes(0, SEND - HALO + k, n)
-        b0[pl.ds(k, n)] = planes(1, SEND - HALO + k, n)
-
-    chunks(HALO, HALO + own_n, spread)
-    for which, ref, pad in ((0, c0, 1), (1, b0, 0)):
+    def spread(which, ref, pad):
+        def body(k, n):
+            ref[pl.ds(pad + k, n)] = planes(which, SEND - HALO + k, n)
+
+        chunks(HALO, HALO + own_n, body)
         ref[pad : pad + HALO] = planes(which, from_lo + SEND - HALO, HALO)
         hi = pad + HALO + own_n
         ref[hi : hi + HALO] = planes(which, from_hi + SEND + own_n, HALO)
+
+    spread(0, c0, 1)
 
     def pairs(ref, k, step):
         v = ref[pl.ds(k, 2 * step)].reshape(step, 2, nd, lanes)
@@ -335,6 +345,12 @@
     level(c0, Z0, HALO, own_n, 1.0, m0, x0, w0, y0, z0, d0, i0)
     level(c1, Z1, H1, L1, 0.25, m1, x1, w1, y1, z1, d1, i1)
     level(c2, Z2, 1, L2, 0.0625, m2, None, None, None, z2, d2, None)
+
+    for c in sources:
+        c.wait()
+    states = deal(2, 2, st_send, st_recv)
+    states_z = beyond(2, 2 * groups)
+    spread(1, b0, 0)
 
     low[mine, 0] = d2[1 : 1 + L2]
     low[mine, 1] = z2[1 : 1 + L2]
@@ -571,9 +587,10 @@
                 jax.ShapeDtypeStruct((cx, cy, cz), F32),
                 jax.ShapeDtypeStruct((cx, cy // n_z), F32),
             ),
-            in_specs=[vm] * 5,
+            in_specs=[pl.BlockSpec(memory_space=pl.ANY)] * 3 + [vm] * 2,
             out_specs=(vm, vm),
             scratch_shapes=[
+                V(cx, cy, cz), V(cx, cy, cz), V(cx, cy, cz), D(3),
                 V(4, cz + 2 * SEND, lanes),
                 V(nd, 4, own + 4 * SEND, lanes),
                 pln(Z0 + 2), pln(Z0), pln(Z0), pln(Z0), pln(Z0 + 1), pln(Z0), pln(Z0), pln(Z0),
@@ -587,7 +604,7 @@
                 V(2, H1, nd, lanes), V(2, H1, nd, lanes),
                 V(3, 3, nd, lanes), V(3, 3, nd, lanes),
                 V(nd, own + 8, lanes), V(parts_n, own + 8, lanes), V(n_z, 8, lanes),
-                D(4 * nd // parts_n), D(2 * nd), D(nd), D(nd), D(nd), D(nd),
+                D(4 * nd // parts_n), D(2 * nd), D(nd), D(nd), D(nd), D(nd), D(nd), D(nd),
                 D(nd), D(nd), D(nd), D(nd),
                 D(4), D(4), D(n_z + 2), D(n_z + 2), D(nd), D(nd), D(n_z), D(n_z),
             ],

time: 44.2 us -> 45.1 us (1.020)
  Pallas kernels: 40.6 us -> 41.4 us
    pallas_call x1, Pallas kernels: 40.6 us -> 41.4 us  [per_device(): pl.pallas_call(functools.partial(kernel, n_x, n_y, n_z, cx, cy, cz, cz *...]
where the time goes in v6:
time: 45.1 us; the launch traced here: 44.8 us
  Pallas kernels  41.4 us (92%)
  local copies, waits for them, and re-layouts  2.8 us (6%)
  between operations  0.64 us (1%)
    pallas_call x1, Pallas kernels, per_device(): pl.pallas_call(functools.partial(kernel, n_x, n_y, n_z, cx, cy, cz, cz *...  41.4 us
    unnamed x1, local copies, waits for them, and re-layouts  1.47 us
    pallas_call x1, local copies, waits for them, and re-layouts, per_device(): pl.pallas_call(functools.partial(kernel, n_x, n_y, n_z, cx, cy, cz, cz *...  1.33 us

profile of v6, /device:TPU:0, one launch (start us, length us, event | category | flops | bytes accessed | tf_op | source)
XLA Modules:
  0.0 44.8 jit_solution(250364211780623320)
XLA Ops:
  0.6 41.4 %shard_map.68 = (f32[8,16,128]{2,1,0:T(8,128)}, f32[8,4]{1,0:T(8,128)}) custom-call(f32[8,16,128]{2,1,0:T(8,128)} %source_in.1, f32[8,16,128]{2,1,0:T(8,128)} %state_in.1, f32[8,16,128]{2,1,0:T(8,128)} %logc_in.1, f32[8,16]{1,0:T(8,128)} %lat_ref.1, s32[1,1,4]{2,1,0:T(1,128)} %owners_ref.1), custom_call_target="tpu_custom_call" | custom-call | flops 100000000 | bytes 400000 | tf_op jit(solution)/shard_map/pallas_call | solution.py:584
  42.0 1.3 %copy.7 = f32[8,4]{0,1:T(4,128)} copy(f32[8,4]{1,0:T(8,128)} %get-tuple-element.3) | data formatting | bytes 256 | tf_op jit(solution)/shard_map/pallas_call | solution.py:584
  43.3 1.5 %copy.9 = f32[8,16,128]{2,1,0:T(8,128)} copy(f32[8,16,128]{2,1,0:T(8,128)} %get-tuple-element.6) | data formatting | bytes 131072

commit v7 on v5

--- a/solution.py
+++ b/solution.py
@@ -24,8 +24,8 @@
     c0, x0, w0, y0, z0, d0, i0, b0, va, vb,
     c1, x1, w1, y1, z1, d1, i1, b1, ma, mb,
     c2, z2, d2, low, rlow, fac, spike, corr,
-    s0, iface, sides, mid_lo, mid_hi, spk_lo, spk_hi, outs, fin, part,
-    z_send, z_recv, main_send, main_recv, st_send, st_recv,
+    s0, iface, sides, mstage, mid_lo, mid_hi, spk_lo, spk_hi, outs, fin, part,
+    z_send, z_recv, main_send, main_recv,
     low_send, low_recv, r_send, r_recv,
     mid_send, mid_recv, if_send, if_recv, fin_send, fin_recv, pt_send, pt_recv,
 ):
@@ -106,49 +106,47 @@
         c.start()
         return c
 
-    def window(first, part):
+    def window(part):
         at = pl.multiple_of(part * own_n, 8)
-        return ext.at[pl.ds(first, 2), pl.ds(at, WIN)]
-
-    def deal(first, ssem, rsem):
+        return ext.at[:, pl.ds(at, WIN)]
+
+    def deal(ssem, rsem):
         sent = []
         for k in range(1, nd):
             part_of = lax.rem(lax.rem(me + k, nd), parts_n)
-            sent.append(copy(window(first, part_of), gath.at[me, pl.ds(first, 2), pl.ds(0, WIN)],
+            sent.append(copy(window(part_of), gath.at[me, :, pl.ds(0, WIN)],
                              ssem.at[k], rsem.at[k], place(k, gz)))
         return sent
 
-    def beyond(first, at):
+    def beyond():
         sent = []
         for i in range(groups):
             for end, row, z, to in (
                 (0, cz_len, up, i * parts_n), (1, SEND, down, (i + 1) * parts_n - 1),
             ):
                 sent.append(copy(
-                    ext.at[pl.ds(first, 2), pl.ds(row, SEND)],
-                    gath.at[me, pl.ds(first, 2), pl.ds(WIN + end * SEND, SEND)],
-                    z_send.at[at + 2 * i + end], z_recv.at[at * nd // 2 // groups + me],
+                    ext.at[:, pl.ds(row, SEND)],
+                    gath.at[me, :, pl.ds(WIN + end * SEND, SEND)],
+                    z_send.at[2 * i + end], z_recv.at[me],
                     (to // n_y, to % n_y, z)))
         return sent
 
-    def beyond_wait(first, at, sent):
+    def beyond_wait(sent):
         for c in sent:
             c.wait_send()
 
         def arrive(end):
             for d in range(nd):
                 pltpu.make_async_remote_copy(
-                    src_ref=ext.at[pl.ds(first, 2), pl.ds(0, SEND)],
-                    dst_ref=gath.at[d, pl.ds(first, 2), pl.ds(WIN + end * SEND, SEND)],
-                    send_sem=z_send.at[0], recv_sem=z_recv.at[at * nd // 2 // groups + d],
+                    src_ref=ext.at[:, pl.ds(0, SEND)],
+                    dst_ref=gath.at[d, :, pl.ds(WIN + end * SEND, SEND)],
+                    send_sem=z_send.at[0], recv_sem=z_recv.at[d],
                     device_id=place(1, gz), device_id_type=MESH,
                 ).wait_recv()
 
         pl.when(mine == 0)(lambda: arrive(0))
         pl.when(mine == parts_n - 1)(lambda: arrive(1))
 
-    main = deal(0, main_send, main_recv)
-    main_z = beyond(0, 0)
     ext[2, SEND : SEND + cz_len, :] = rows_of(state_ref)
     ext[2, 0:SEND, :] = jnp.zeros((SEND, lanes), F32)
     ext[2, SEND + cz_len :, :] = jnp.zeros((SEND, lanes), F32)
@@ -165,8 +163,8 @@
     flags = jnp.concatenate(flags, axis=0)
     for j in range(0, cz_len + 2 * SEND, SEND):
         ext[3, j : j + SEND, :] = flags
-    states = deal(2, st_send, st_recv)
-    states_z = beyond(2, 2 * groups)
+    main = deal(main_send, main_recv)
+    main_z = beyond()
     gath[me, :, 0:WIN, :] = ext[:, pl.ds(pl.multiple_of(mine * own_n, 8), WIN), :]
     from_lo = (parts_n - 1 - mine) // (parts_n - 1) * WIN
     from_hi = mine // (parts_n - 1) * (2 * SEND)
@@ -302,7 +300,7 @@
 
     for c in main:
         c.wait()
-    beyond_wait(0, 0, main_z)
+    beyond_wait(main_z)
     flat = gath.reshape(nd * 4 * HIGH, lanes)
 
     def planes(which, start, n):
@@ -367,11 +365,12 @@
     sweep(ma, mb, b1, 3, Z1 - 3, *mid, i1)
     sweep(mb, ma, b1, 4, Z1 - 4, *mid, i1)
 
+    for end, row in ((0, L1), (1, H1)):
+        mstage[end, 0] = ma[1 + row : 1 + row + H1]
+        mstage[end, 1] = b1[row : row + H1]
     mids = [
-        copy(ma.at[pl.ds(1 + L1, H1)], mid_lo.at[0], mid_send.at[0], mid_recv.at[0], along(1)),
-        copy(b1.at[pl.ds(L1, H1)], mid_lo.at[1], mid_send.at[1], mid_recv.at[1], along(1)),
-        copy(ma.at[pl.ds(1 + H1, H1)], mid_hi.at[0], mid_send.at[2], mid_recv.at[2], along(-1)),
-        copy(b1.at[pl.ds(H1, H1)], mid_hi.at[1], mid_send.at[3], mid_recv.at[3], along(-1)),
+        copy(mstage.at[0], mid_lo, mid_send.at[0], mid_recv.at[0], along(1)),
+        copy(mstage.at[1], mid_hi, mid_send.at[1], mid_recv.at[1], along(-1)),
     ]
 
     rlow[mine] = residual(ma, b1, d1, H1, L2, *mid)
@@ -408,9 +407,6 @@
         p = spike[1, k] * fac[2, k] + f * p
         q = f * q
         spike[1, k], spike[2, k] = p, q
-    for c in states:
-        c.wait()
-    beyond_wait(2, 2 * groups, states_z)
     cut_plane = planes(3, SEND + gz, 1)[0]
     for c in rights:
         c.wait()
@@ -584,12 +580,12 @@
                 V(parts_n, 2, L2, nd, lanes), V(parts_n, L2, nd, lanes),
                 V(3, NL, nd, lanes), V(3, NL, nd, lanes), pln(NL + 6),
                 pln(own + 2), V(n_z, 7, nd, lanes), V(n_z, 2, nd, lanes),
-                V(2, H1, nd, lanes), V(2, H1, nd, lanes),
+                V(2, 2, H1, nd, lanes), V(2, H1, nd, lanes), V(2, H1, nd, lanes),
                 V(3, 3, nd, lanes), V(3, 3, nd, lanes),
                 V(nd, own + 8, lanes), V(parts_n, own + 8, lanes), V(n_z, 8, lanes),
-                D(4 * nd // parts_n), D(2 * nd), D(nd), D(nd), D(nd), D(nd),
+                D(2 * nd // parts_n), D(nd), D(nd), D(nd),
                 D(nd), D(nd), D(nd), D(nd),
-                D(4), D(4), D(n_z + 2), D(n_z + 2), D(nd), D(nd), D(n_z), D(n_z),
+                D(2), D(2), D(n_z + 2), D(n_z + 2), D(nd), D(nd), D(n_z), D(n_z),
             ],
             compiler_params=pltpu.CompilerParams(
                 collective_id=0, has_side_effects=True, vmem_limit_bytes=56 * 1024 * 1024

time: 44.2 us -> 46.2 us (1.045)
  Pallas kernels: 40.6 us -> 42.5 us
    pallas_call x1, Pallas kernels: 40.6 us -> 42.5 us  [per_device(): pl.pallas_call(functools.partial(kernel, n_x, n_y, n_z, cx, cy, cz, cz *...]
where the time goes in v7:
time: 46.2 us; the launch traced here: 45.9 us
  Pallas kernels  42.5 us (92%)
  local copies, waits for them, and re-layouts  2.8 us (6%)
  between operations  0.64 us (1%)
    pallas_call x1, Pallas kernels, per_device(): pl.pallas_call(functools.partial(kernel, n_x, n_y, n_z, cx, cy, cz, cz *...  42.5 us
    unnamed x1, local copies, waits for them, and re-layouts  1.47 us
    pallas_call x1, local copies, waits for them, and re-layouts, per_device(): pl.pallas_call(functools.partial(kernel, n_x, n_y, n_z, cx, cy, cz, cz *...  1.33 us

profile of v7, /device:TPU:0, one launch (start us, length us, event | category | flops | bytes accessed | tf_op | source)
XLA Modules:
  0.0 45.9 jit_solution(1595249138394685599)
XLA Ops:
  0.6 42.5 %shard_map.68 = (f32[8,16,128]{2,1,0:T(8,128)}, f32[8,4]{1,0:T(8,128)}) custom-call(f32[8,16,128]{2,1,0:T(8,128)} %source_ref.1, f32[8,16,128]{2,1,0:T(8,128)} %state_ref.1, f32[8,16,128]{2,1,0:T(8,128)} %logc_ref.1, f32[8,16]{1,0:T(8,128)} %lat_ref.1, s32[1,1,4]{2,1,0:T(1,128)} %owners_ref.1), custom_call_target="tpu_custom_call" | custom-call | flops 100000000 | bytes 400000 | tf_op jit(solution)/shard_map/pallas_call | solution.py:564
  43.1 1.3 %copy.7 = f32[8,4]{0,1:T(4,128)} copy(f32[8,4]{1,0:T(8,128)} %get-tuple-element.3) | data formatting | bytes 256 | tf_op jit(solution)/shard_map/pallas_call | solution.py:564
  44.5 1.5 %copy.9 = f32[8,16,128]{2,1,0:T(8,128)} copy(f32[8,16,128]{2,1,0:T(8,128)} %get-tuple-element.6) | data formatting | bytes 131072
